TPU v7x, 32 devices: a whole 2x2x4 slice. The times are simulated.
32 devices in a mesh: dp: 8 (over y, x, core), tp: 4 (over z).
Axes of the slice: x: 2, y: 2, z: 4, core: 2. Of those that a mesh axis runs over, the one named last changes fastest.
Arguments:
- tokens: bfloat16 [8, 1024, 768], P('dp', 'tp')
- w_qkv: bfloat16 [768, 2304], replicated, may hold values from -0.21875 to 0.21875
- bias_query: bfloat16 [768], replicated, may hold values from -1.5 to 1.5
- bias_value: bfloat16 [768], replicated, may hold values from -1.5 to 1.5
- w_out: bfloat16 [768, 768], replicated, may hold values from -1.25 to 1.25
- bias_out: bfloat16 [768], replicated, may hold values from -1.5 to 1.5
- gain_attn: bfloat16 [768], replicated, may hold values from 0.25 to 1.75
- shift_attn: bfloat16 [768], replicated, may hold values from -1.5 to 1.5
- w_in: bfloat16 [768, 3072], P(None, 'tp'), may hold values from -0.21875 to 0.21875
- bias_in: bfloat16 [3072], P('tp'), may hold values from -1.5 to 1.5
- w_back: bfloat16 [3072, 768], P('tp'), may hold values from -0.109375 to 0.109375
- bias_back: bfloat16 [768], replicated, may hold values from -1.5 to 1.5
- gain_ffn: bfloat16 [768], replicated, may hold values from 0.25 to 1.75
- shift_ffn: bfloat16 [768], replicated, may hold values from -1.5 to 1.5
- random_blocks: int32 [8, 12, 16, 3], P('dp'), may hold values from 1 to 14, as said below
- cotangent: bfloat16 [8, 1024, 768], P('dp', 'tp'), may hold values from -6 to 6
Outputs:
- layer_out: bfloat16 [8, 1024, 768], P('dp', 'tp')
- grad_tokens: bfloat16 [8, 1024, 768], P('dp', 'tp')
- grad_w_qkv: float32 [768, 2304], replicated
- grad_bias_query: float32 [768], replicated
- grad_bias_value: float32 [768], replicated
- grad_w_out: float32 [768, 768], replicated
- grad_bias_out: float32 [768], replicated
- grad_gain_attn: float32 [768], replicated
- grad_shift_attn: float32 [768], replicated
- grad_w_in: float32 [768, 3072], P(None, 'tp')
- grad_bias_in: float32 [3072], P('tp')
- grad_w_back: float32 [3072, 768], P('tp')
- grad_bias_back: float32 [768], replicated
- grad_gain_ffn: float32 [768], replicated
- grad_shift_ffn: float32 [768], replicated
Inputs may be any that keep to these rules, and one draw needn't show every extreme that they name: `random_blocks`: for each sequence, head and query block i, the 3 entries are different block numbers, none of them 0, 15, i - 1, i or i + 1.
All inputs are finite; a program needn't handle non-finite values.
Results may differ from a plain program's by a relative error of at most 0.017.
Values may be sent and summed in bfloat16 or wider, within the bound.
No kernel may reach another device: no remote copies, remote signals or barrier semaphores. Data moves between devices by JAX's collectives and lax.ppermute only.
A program may use at most 192 MiB of HBM per device.

v0:
```python
import functools

import jax
import jax.numpy as jnp
from jax import lax
from jax.experimental import pallas as pl
from jax.experimental.pallas import tpu as pltpu
from jax.sharding import PartitionSpec as P

HEADS = 12
BLOCK = 64
HEAD_DIM = 64
TP = 4
GROUP = HEADS // TP
QUARTER = 256
LENGTH = TP * QUARTER
WIDTH = HEADS * HEAD_DIM
GROUP_WIDTH = GROUP * HEAD_DIM
SLOTS = 8
SLICE = WIDTH // SLOTS
VEC_ROWS = 16
CORE, X_BIT, Y_BIT = 1, 2, 4
PLANE_MASKS = (0, X_BIT, Y_BIT, X_BIT | Y_BIT)

epsilon = 1e-05
masked_score = -1e30
score_scale = HEAD_DIM ** (-0.5)
f32 = jnp.float32
bf16 = jnp.bfloat16


def mm(left, right):
    return jnp.dot(left, right, preferred_element_type=f32)


def mm_nt(left, right):
    return lax.dot_general(left, right, (((1,), (1,)), ((), ())), preferred_element_type=f32)


def total(*terms):
    acc = terms[0].astype(f32)
    for term in terms[1:]:
        acc = acc + term.astype(f32)
    return acc


def add_low(*terms):
    return total(*terms).astype(bf16)


def hop(array, dp_mask, z_mask):
    dp_count = lax.axis_size("dp")
    pairs = [
        (d * TP + z, (d ^ dp_mask) * TP + (z ^ z_mask)) for d in range(dp_count) for z in range(TP)
    ]
    return lax.ppermute(array, ("dp", "tp"), pairs)


def place(array):
    dp_count = lax.axis_size("dp")
    pairs = []
    for d in range(dp_count):
        for z in range(TP):
            here = d * TP + z
            away = (d ^ CORE) * TP + (z ^ 2)
            pairs.append((here, here if (d & 1) == z // 2 else away))
    return lax.ppermute(array, ("dp", "tp"), pairs)


def piece_kernel(info, w_in_hbm, w_back_ref, bias_ref, piece_ref, flip_scr, sem):
    start = pl.multiple_of(info[1] * SLICE, SLICE)
    copy = pltpu.make_async_copy(
        w_in_hbm.at[pl.ds(start, SLICE), :], piece_ref.at[pl.ds(0, SLICE), :], sem
    )
    copy.start()
    flip_scr[...] = w_back_ref[...].T
    piece_ref[SLICE : 2 * SLICE, :] = flip_scr[pl.ds(start, SLICE), :]
    bias = bias_ref[...].astype(f32).reshape(1, WIDTH)
    piece_ref[2 * SLICE :, :] = jnp.broadcast_to(bias, (VEC_ROWS, WIDTH)).astype(bf16)
    copy.wait()


def group_kernel(info, w_ref, bias_query_ref, bias_value_ref, w_out, b_out):
    bias_query = bias_query_ref[...].astype(f32).reshape(1, WIDTH)
    bias_value = bias_value_ref[...].astype(f32).reshape(1, WIDTH)
    b_out[...] = jnp.zeros_like(b_out)
    for g in range(TP):

        @pl.when(info[0] == g)
        def _(g=g):
            cols = slice(g * GROUP_WIDTH, (g + 1) * GROUP_WIDTH)
            for kind in range(3):
                lo = kind * GROUP_WIDTH
                w_out[:, lo : lo + GROUP_WIDTH] = w_ref[:, kind * WIDTH :][:, cols]
            b_out[:, :GROUP_WIDTH] = bias_query[:, cols]
            b_out[:, 2 * GROUP_WIDTH :] = bias_value[:, cols]


def block_bias(quarter, native, random_refs, head, chunk):
    shape = (LENGTH // BLOCK, QUARTER)
    row = lax.broadcasted_iota(jnp.int32, shape, 0)
    lane_block = lax.broadcasted_iota(jnp.int32, shape, 1) // BLOCK
    key_block = ((row // TP) ^ quarter) * TP + (row % TP)
    base = TP * (quarter ^ chunk)
    query_block = base + lane_block
    last = LENGTH // BLOCK - 1
    allowed = (key_block == 0) | (key_block == last)
    allowed |= (query_block == 0) | (query_block == last)
    allowed |= jnp.abs(key_block - query_block) <= 1
    for pick in range(3):
        chosen = jnp.zeros(shape, jnp.int32)
        for b in range(TP):
            at = (head * (LENGTH // BLOCK) + base + b) * 3 + pick
            value = jnp.where(native == 1, random_refs[0][at], random_refs[1][at])
            chosen = jnp.where(lane_block == b, value, chosen)
        allowed |= key_block == chosen
    return jnp.where(allowed, 0.0, masked_score).astype(f32)


def biased(scores, bias):
    blocks = LENGTH // BLOCK
    spread = scores.reshape(blocks, BLOCK, QUARTER) + bias.reshape(blocks, 1, QUARTER)
    return spread.reshape(LENGTH, QUARTER)


PACKED = QUARTER + QUARTER // 2


def pack_heads(ref, row, pieces):
    end = row + QUARTER
    ref[row:end, 0:64] = pieces[0]
    ref[row:end, 64:128] = pieces[1]
    ref[end : row + PACKED, 0:64] = pieces[2][: QUARTER // 2]
    ref[end : row + PACKED, 64:128] = pieces[2][QUARTER // 2 :]


def unpack_heads(ref, row):
    end = row + QUARTER
    third = jnp.concatenate([ref[end : row + PACKED, 0:64], ref[end : row + PACKED, 64:128]], axis=0)
    return [ref[row:end, 0:64], ref[row:end, 64:128], third]


def attention_kernel(info, rnd_own, rnd_other, t0, t1, t2, t3, w_ref, b_ref, a0, a13, a2, *rest):
    heads, lse_ref, outs = rest[:9], rest[9], rest[10]
    ones = jnp.ones((8, LENGTH), bf16)
    quarter, native = info[0], info[4]
    for slot, t_ref in enumerate((t0, t1, t2, t3)):
        rows = pl.ds(slot * QUARTER, QUARTER)
        proj = mm(t_ref[...], w_ref[...]) + b_ref[...]
        for h in range(GROUP):
            for kind in range(3):
                lo = kind * GROUP_WIDTH + h * HEAD_DIM
                piece = proj[:, lo : lo + HEAD_DIM].astype(bf16)
                if kind == 0:
                    piece = (piece.astype(f32) * score_scale).astype(bf16)
                heads[3 * h + kind][rows, :] = piece
    for h in range(GROUP):
        q_ref, k_ref, v_ref = heads[3 * h : 3 * h + 3]
        keys = k_ref[...]
        values_t = jnp.concatenate([v_ref[...].T, ones], axis=0)

        def chunk_step(chunk, carry, h=h, q_ref=q_ref, keys=keys, values_t=values_t):
            rows = pl.ds(pl.multiple_of(chunk * QUARTER, QUARTER), QUARTER)
            scores = mm_nt(keys, q_ref[rows, :])
            head = quarter * GROUP + h
            scores = biased(scores, block_bias(quarter, native, (rnd_own, rnd_other), head, chunk))
            row_max = jnp.max(scores, axis=0, keepdims=True)
            probs = jnp.exp(scores - row_max)
            out_t = mm(values_t, probs.astype(bf16))
            row_sum = out_t[HEAD_DIM : HEAD_DIM + 1]
            out_t = out_t[:HEAD_DIM] / row_sum
            outs[h, rows, :] = out_t.T.astype(bf16)
            lse_ref[pl.ds(h * TP + chunk, 1), :] = row_max + jnp.log(row_sum)
            return carry

        lax.fori_loop(0, TP, chunk_step, 0, unroll=True)
    for slot, (a_ref, row) in enumerate(((a0, 0), (a13, 0), (a2, 0), (a13, PACKED))):
        rows = slice(slot * QUARTER, (slot + 1) * QUARTER)
        pack_heads(a_ref, row, [outs[h, rows, :] for h in range(GROUP)])


def attention_back_kernel(
    h, info, rnd_own, rnd_other, q_ref, k_ref, v_ref, lse_ref, g0, g1, g2, g3, out_ref, sums_ref, do_scr, dk_scr, dv_scr, dq_scr
):
    quarter, native = info[0], info[4]
    for slot, g_ref in enumerate((g0, g1, g2, g3)):
        do_scr[slot * QUARTER : (slot + 1) * QUARTER, :] = unpack_heads(g_ref, 0)[h]
    keys = k_ref[...]
    keys_t = keys.T
    values = v_ref[...]
    dk_scr[...] = jnp.zeros_like(dk_scr)
    dv_scr[...] = jnp.zeros_like(dv_scr)

    def chunk_step(chunk, carry):
        rows = pl.ds(pl.multiple_of(chunk * QUARTER, QUARTER), QUARTER)
        queries = q_ref[rows, :]
        grad_out = do_scr[rows, :]
        scores = mm_nt(keys, queries)
        head = quarter * GROUP + h
        bias = block_bias(quarter, native, (rnd_own, rnd_other), head, chunk)
        probs = jnp.exp(biased(scores, bias - lse_ref[pl.ds(h * TP + chunk, 1), :]))
        grad_probs = mm_nt(values, grad_out)
        delta = jnp.sum(probs * grad_probs, axis=0, keepdims=True)
        grad_scores = (probs * (grad_probs - delta)).astype(bf16)
        dv_scr[...] += mm(probs.astype(bf16), grad_out)
        dk_scr[...] += mm(grad_scores, queries)
        dq_t = mm(keys_t, grad_scores) * score_scale
        dq_scr[rows, :] = dq_t.T
        return carry

    lax.fori_loop(0, TP, chunk_step, 0, unroll=True)
    for n, scr in enumerate((dq_scr, dk_scr, dv_scr)):
        out_ref[:, n * HEAD_DIM : (n + 1) * HEAD_DIM] = scr[...].astype(bf16)
    sums_ref[...] = jnp.zeros_like(sums_ref)
    sums_ref[0:1, :] = jnp.sum(out_ref[...].astype(f32), axis=0, keepdims=True)


PIECE = 2 * SLICE + VEC_ROWS
ROOT = 0.7978845608028654
CUBE = 0.044715 * ROOT


def held_kernel(own, by_x, by_y, third, third_x, third_y, out):
    for q in range(2):
        for p, ref in enumerate((own, by_x, by_y)):
            at = (4 * q + p) * PIECE
            out[at : at + PIECE] = ref[q * PIECE : (q + 1) * PIECE]
        at = (4 * q + 3) * PIECE
        out[at : at + CUT] = third_y[PIECE + q * CUT : PIECE + (q + 1) * CUT]
        out[at + CUT : at + PIECE] = third_x[PIECE + q * (PIECE - CUT) : PIECE + (q + 1) * (PIECE - CUT)]
    for p, ref in enumerate((third, third_x, third_y)):
        at = (8 + p) * PIECE
        out[at : at + PIECE] = ref[:PIECE]


def assemble_kernel(info, held, other, last_in, last_back, other_last, w_out_ref, w_in_s, w_back_s, w_out_s, bias_s):
    quarter, mine = info[0], info[1]
    for slot in range(TP):
        start = pl.multiple_of((quarter ^ slot) * GROUP_WIDTH, GROUP_WIDTH)
        w_out_s[slot * GROUP_WIDTH : (slot + 1) * GROUP_WIDTH, :] = w_out_ref[pl.ds(start, GROUP_WIDTH), :]
    for side, main in enumerate((held, other)):
        for q in range(TP - 1):
            for p in range(4):
                start = pl.multiple_of((mine ^ PLANE_MASKS[p] ^ side) * SLICE, SLICE)
                at = (4 * q + p) * PIECE
                if q == TP - 2 and p == 3:
                    left = other_last[:SLICE] if side else last_in[...]
                    right = other_last[SLICE : 2 * SLICE] if side else last_back[:SLICE]
                else:
                    left, right = main[at : at + SLICE], main[at + SLICE : at + 2 * SLICE]
                w_in_s[q, pl.ds(start, SLICE), :] = left
                w_back_s[q, pl.ds(start, SLICE), :] = right
                if p == 0 and side == 0:
                    bias_s[q] = main[at + 2 * SLICE : at + PIECE]


def wait_all(copies):
    for copy in copies:
        copy.wait()


def row(ref):
    return ref[...].astype(f32).reshape(1, WIDTH)


def spread(h):
    centred = h - jnp.mean(h, axis=-1, keepdims=True)
    scale = lax.rsqrt(jnp.mean(centred * centred, axis=-1, keepdims=True) + epsilon)
    return centred * scale, scale


def spread_back(grad, gain, normal, scale):
    weighted = grad * gain
    mean_one = jnp.mean(weighted, axis=-1, keepdims=True)
    mean_two = jnp.mean(weighted * normal, axis=-1, keepdims=True)
    return scale * (weighted - mean_one - normal * mean_two)


def ffn_kernel(info, t_ref, a0, a1, a2, a3, *rest):
    bias_out_ref, gain_one_ref, shift_one_ref, bias_back_ref, gain_two_ref, shift_two_ref, bias_in_ref = rest[:7]
    cot_ref, w_out_s, w_in_ref, w_back_ref, w_in_s, w_back_s, bias_s = rest[7:14]
    lo_ref, first_ref, second_ref, x_ref, gb_ref, act_ref, gp_ref, att_ref, vec_ref = rest[14:]
    for slot, a_ref in enumerate((a0, a1, a2, a3)):
        for h, piece in enumerate(unpack_heads(a_ref, 0)):
            lo = slot * GROUP_WIDTH + h * HEAD_DIM
            att_ref[:, lo : lo + HEAD_DIM] = piece
    first_in = t_ref[...].astype(f32) + (mm(att_ref[...], w_out_s[...]) + row(bias_out_ref))
    first_ref[...] = first_in
    first_norm = spread(first_in)[0] * row(gain_one_ref) + row(shift_one_ref)
    x = first_norm.astype(bf16)
    x_ref[...] = x
    branch = jnp.zeros((QUARTER, WIDTH), f32)
    for q in range(TP):
        cols = slice(q * WIDTH, (q + 1) * WIDTH)
        bias_q = bias_s[q - 1, 0:1, :].astype(f32) if q else row(bias_in_ref)
        pre = mm(x, w_in_s[q - 1] if q else w_in_ref[...]) + bias_q
        square = pre * pre
        half = 0.5 + 0.5 * jnp.tanh(pre * (ROOT + CUBE * square))
        wide_act = pre * half
        act = wide_act.astype(bf16)
        act_ref[:, cols] = act
        gp_ref[:, cols] = half + wide_act * (1.0 - half) * (2.0 * ROOT + 6.0 * CUBE * square)
        branch = branch + (mm_nt(act, w_back_s[q - 1]) if q else mm(act, w_back_ref[...]))
    second_in = first_norm + branch + row(bias_back_ref)
    normal_two, scale_two = spread(second_in)
    lo_ref[...] = (normal_two * row(gain_two_ref) + row(shift_two_ref)).astype(bf16)
    grad_out = cot_ref[...].astype(f32)
    grad_second = spread_back(grad_out, row(gain_two_ref), normal_two, scale_two)
    second_ref[...] = grad_second
    grad_branch = grad_second.astype(bf16)
    gb_ref[...] = grad_branch
    vec_ref[...] = jnp.zeros_like(vec_ref)
    vec_ref[0:1, :] = jnp.sum(grad_out, axis=0, keepdims=True)
    vec_ref[1:2, :] = jnp.sum(grad_out * normal_two, axis=0, keepdims=True)
    vec_ref[2:3, :] = jnp.sum(grad_branch.astype(f32), axis=0, keepdims=True)


def position_mask(position, order):
    mask = 0
    for n, bit in enumerate(order):
        if (position >> (2 - n)) & 1:
            mask |= bit
    return mask


FFN_ORDERS = ((CORE, X_BIT, Y_BIT), (CORE, Y_BIT, X_BIT))


def weight_grads(info, left, right, keep, send, flip_scr, lhs_scr):
    mine = info[1]
    flip_scr[...] = left[...].T
    for n, order in enumerate(FFN_ORDERS):
        for p in range(SLOTS):
            start = pl.multiple_of((mine ^ position_mask(p, order)) * SLICE, SLICE)
            lhs_scr[p * SLICE : (p + 1) * SLICE, :] = flip_scr[pl.ds(start, SLICE), :]
        for pair in range(2):
            q = 2 * n + pair
            product = mm(lhs_scr[...], right[:, q * WIDTH : (q + 1) * WIDTH]).astype(bf16)
            for p in range(SLOTS):
                out = send if p >= SLOTS // 2 else keep
                out[n, p % (SLOTS // 2), pair] = product[p * SLICE : (p + 1) * SLICE, :]


def ffn_back_kernel(info, first_ref, second_ref, gb_ref, gp_ref, gain_one_ref, vec_in, *rest):
    w_out_s, w_in_ref, w_back_ref, w_in_s, w_back_s, x_ref, att_ref = rest[:7]
    g0, g13, g2, gin_ref, vec_ref, keep, send, go_keep, go_send = rest[7:16]
    gpre_ref, flip_scr, lhs_scr = rest[16:]
    grad_branch = gb_ref[...]
    grad_first = second_ref[...]
    vec_ref[...] = vec_in[...]
    for q in range(TP):
        cols = slice(q * WIDTH, (q + 1) * WIDTH)
        grad_act = mm(grad_branch, w_back_s[q - 1]) if q else mm_nt(grad_branch, w_back_ref[...])
        grad_pre = (grad_act * gp_ref[:, cols]).astype(bf16)
        gpre_ref[:, cols] = grad_pre
        vec_ref[pl.ds(6 + (info[2] ^ q), 1), :] = jnp.sum(grad_pre.astype(f32), axis=0, keepdims=True)
        grad_first = grad_first + mm_nt(grad_pre, w_in_s[q - 1] if q else w_in_ref[...])
    normal_one, scale_one = spread(first_ref[...])
    vec_ref[3:4, :] = jnp.sum(grad_first, axis=0, keepdims=True)
    vec_ref[4:5, :] = jnp.sum(grad_first * normal_one, axis=0, keepdims=True)
    grad_in = spread_back(grad_first, row(gain_one_ref), normal_one, scale_one)
    gin_ref[...] = grad_in
    grad_mixed = grad_in.astype(bf16)
    vec_ref[5:6, :] = jnp.sum(grad_mixed.astype(f32), axis=0, keepdims=True)
    grad_att = mm_nt(grad_mixed, w_out_s[...]).astype(bf16)
    for slot, (g_ref, row_at) in enumerate(((g0, 0), (g13, 0), (g2, 0), (g13, PACKED))):
        lo = slot * GROUP_WIDTH
        pack_heads(
            g_ref, row_at, [grad_att[:, lo + h * HEAD_DIM : lo + (h + 1) * HEAD_DIM] for h in range(GROUP)]
        )
    weight_grads(info, x_ref, gpre_ref, keep, send, flip_scr, lhs_scr)
    product = mm(grad_mixed.T, att_ref[...]).astype(bf16)
    go_keep[...] = product[:, : 2 * GROUP_WIDTH]
    go_send[...] = product[:, 2 * GROUP_WIDTH :]


ORDER_LA = (4, 2, 1)
ORDER_LB = (2, 4, 1)


HALF = WIDTH // 2
HELD = SLOTS // 2 * SLICE


def flip_kernel(t0, t1, t2, t3, out_ref):
    for slot, t_ref in enumerate((t0, t1, t2, t3)):
        out_ref[:, slot * QUARTER : (slot + 1) * QUARTER] = t_ref[...].T


def qkv_grad_kernel(
    info, tokens_t, gh0, gh1, gh2, go_own, go_near, vec_ref, s0, s1, s2, la_keep, la_send, lb_keep, lb_send, out_scr
):
    quarter, here = info[0], info[3]
    for h, gh_ref in enumerate((gh0, gh1, gh2)):
        product = mm(tokens_t[...], gh_ref[...]).astype(bf16)
        for kind in range(3):
            lo = kind * GROUP_WIDTH + h * HEAD_DIM
            out_scr[:, lo : lo + HEAD_DIM] = product[:, kind * HEAD_DIM : (kind + 1) * HEAD_DIM]
    add_to(out_scr.at[:, 3 * GROUP_WIDTH :], go_own[...], go_near[...])
    for keep, send, order, lo in (
        (la_keep, la_send, ORDER_LA, 0),
        (lb_keep, lb_send, ORDER_LB, HALF),
    ):
        for p in range(SLOTS):
            start = pl.multiple_of((here ^ position_mask(p, order)) * SLICE, SLICE)
            out = send if p >= SLOTS // 2 else keep
            row = p % (SLOTS // 2) * SLICE
            out[row : row + SLICE, :] = out_scr[pl.ds(start, SLICE), lo : lo + HALF]
    placed = []
    for kind in (0, 2):
        cols = slice(kind * HEAD_DIM, (kind + 1) * HEAD_DIM)
        piece = jnp.concatenate([sums[0:1, cols] for sums in (s0, s1, s2)], axis=1)
        placed.append(
            jnp.concatenate([jnp.where(quarter == g, piece, 0.0) for g in range(TP)], axis=1)
        )
    vectors = jnp.concatenate([vec_ref[0:10, :]] + placed + [vec_ref[12:VEC_ROWS, :]], axis=0)
    vectors = vectors.astype(bf16)
    for out in (la_keep, la_send, lb_keep, lb_send):
        out[HELD : HELD + VEC_ROWS, :] = vectors[:, :HALF]
        out[HELD + VEC_ROWS :, :] = vectors[:, HALF:]


def token_grad_kernel(gh0, gh1, gh2, w_ref, keep_ref, send_ref, all_scr):
    for h, gh_ref in enumerate((gh0, gh1, gh2)):
        for kind in range(3):
            lo = kind * GROUP_WIDTH + h * HEAD_DIM
            all_scr[:, lo : lo + HEAD_DIM] = gh_ref[:, kind * HEAD_DIM : (kind + 1) * HEAD_DIM]
    half = LENGTH // 2
    send_ref[...] = mm_nt(all_scr[half:, :], w_ref[...]).astype(bf16)
    keep_ref[...] = mm_nt(all_scr[:half, :], w_ref[...]).astype(bf16)


FFN_AT = 16 * SLICE + VEC_ROWS
HALF_GROUPS = TP // 2 * GROUP_WIDTH


def write_half(info, side, plane, qkv_hbm, out_hbm, w_in_hbm, qkv_scr, out_scr, w_in_scr, sems):
    quarter, mine, here = info[0], info[1], info[3]
    core = (quarter >> 1) ^ side
    first_col = core * HALF_GROUPS
    copies = []

    def send(source, target):
        copies.append(pltpu.make_async_copy(source, target, sems.at[len(copies)]))
        copies[-1].start()

    def piece(at, cols):
        block_off = here ^ at
        xy = ((block_off >> 2) & 1) + (block_off & 2)
        parts = []
        for group in range(2):
            nth = xy * 4 + ((quarter & 1) ^ group) + 2 * (block_off & 1)
            parts.append(plane[pl.ds(pl.multiple_of(nth * SLICE, SLICE), SLICE), cols])
        return jnp.concatenate(parts, axis=1).astype(f32)

    for chunk in range(SLOTS // 2):
        rows = pl.ds(2 * chunk * SLICE, 2 * SLICE)
        for kind in range(3):
            cols = pl.ds(kind * HALF_GROUPS, HALF_GROUPS)
            for at in (2 * chunk, 2 * chunk + 1):
                qkv_scr[at * SLICE : (at + 1) * SLICE, kind * HALF_GROUPS : (kind + 1) * HALF_GROUPS] = piece(
                    at, slice(kind * GROUP_WIDTH, (kind + 1) * GROUP_WIDTH)
                )
            to = pl.ds(pl.multiple_of(kind * WIDTH + first_col, 128), HALF_GROUPS)
            send(qkv_scr.at[rows, cols], qkv_hbm.at[rows, to])
        at = 2 * chunk + core
        mask = mine ^ at
        nth = (((mask >> 1) & 1) + ((mask >> 2) & 1) * 2) * 2
        start = pl.multiple_of(FFN_AT + nth * SLICE, VEC_ROWS)
        here_rows = pl.ds(chunk * SLICE, SLICE)
        w_in_scr[here_rows, :] = plane[pl.ds(start, SLICE), :].astype(f32)
        send(w_in_scr.at[here_rows, :], w_in_hbm.at[pl.ds(pl.multiple_of(at * SLICE, SLICE), SLICE), :])
    cols = slice(3 * GROUP_WIDTH, 4 * GROUP_WIDTH)
    out_scr[...] = jnp.concatenate([piece(at, cols) for at in range(SLOTS)], axis=0).T
    send(out_scr, out_hbm.at[pl.ds(pl.multiple_of(first_col, HALF_GROUPS), HALF_GROUPS), :])
    return copies


def first_half_kernel(info, plane, low_tokens, low_out, qkv_hbm, out_hbm, w_in_hbm, layer_out, token_out, *scratch):
    whole = [
        pltpu.make_async_copy(low_out, layer_out, scratch[4].at[0]),
        pltpu.make_async_copy(low_tokens, token_out, scratch[4].at[1]),
    ]
    for copy in whole:
        copy.start()
    wait_all(write_half(info, 0, plane, qkv_hbm, out_hbm, w_in_hbm, *scratch[:4]) + whole)


def second_half_kernel(info, plane, other, _qkv, _out, _w_in, qkv_hbm, out_hbm, w_in_hbm, w_back_hbm, *rest):
    vec_outs, scratch = rest[:9], rest[9:]
    mine, z_here = info[1], info[2]
    flip_scr, back_scr, sem = scratch[4:]
    for core in range(2):

        @pl.when((mine & 1) == core)
        def _(core=core):
            for at in range(SLOTS):
                mask = mine ^ at
                nth = (((mask >> 1) & 1) + ((mask >> 2) & 1) * 2) * 2 + 1
                start = pl.multiple_of(FFN_AT + nth * SLICE, VEC_ROWS)
                ref = plane if (at & 1) == core else other
                flip_scr[at * SLICE : (at + 1) * SLICE, :] = ref[pl.ds(start, SLICE), :].astype(f32)

    back_scr[...] = flip_scr[...].T
    back_copy = pltpu.make_async_copy(back_scr, w_back_hbm, sem)
    back_copy.start()
    copies = write_half(info, 1, other, qkv_hbm, out_hbm, w_in_hbm, *scratch[:4])
    vec_rows = slice(16 * SLICE, FFN_AT)
    vectors = total(plane[vec_rows, :], other[vec_rows, :])
    bias_in = jnp.zeros((1, WIDTH), f32)
    for q in range(TP):
        bias_in = jnp.where(z_here == q, vectors[6 + q : 7 + q, :], bias_in)
    for out, n in zip(vec_outs[:8], (0, 1, 2, 3, 4, 5, 10, 11)):
        out[...] = vectors[n]
    vec_outs[8][...] = bias_in[0]
    wait_all(copies + [back_copy])


def add_to(out, *terms):
    out[...] = add_low(*terms)


def join_kernel(*refs):
    out, at = refs[-1], 0
    for ref in refs[:-1]:
        out[at : at + ref.shape[0]] = ref[...]
        at += ref.shape[0]


def diag_kernel(by_x, by_y, first, second):
    half = first.shape[0]
    first[...] = by_x[:half]
    second[...] = by_y[half:]


CUT = SLICE


def mix_kernel(by_x, by_y, own, to_x, to_y):
    to_x[:PIECE] = own[...]
    to_y[:PIECE] = own[...]
    for n in range(2):
        to_x[PIECE + n * (PIECE - CUT) : PIECE + (n + 1) * (PIECE - CUT)] = by_y[n * PIECE + CUT : (n + 1) * PIECE]
        to_y[PIECE + n * CUT : PIECE + (n + 1) * CUT] = by_x[n * PIECE : n * PIECE + CUT]


def last_mix_kernel(by_x, by_y, to_x, to_y):
    to_x[...] = by_y[CUT:PIECE]
    to_y[...] = by_x[:CUT]


def level_one_kernel(keep, other, first, second):
    add_to(first, keep[0, 2:], other[0, 2:])
    add_to(second, keep[1, 2:], other[1, 2:])


def middle_kernel(in_keep, in_other, back_keep, back_other, back_x, back_y, to_x, to_y):
    for n in range(2):
        out = to_y if n else to_x
        for p in range(2):
            for pair in range(2):
                add_to(out.at[2 * p + pair], in_keep[n, 2 + p, pair], in_other[n, 2 + p, pair])
    for pair in range(2):
        add_to(to_y.at[4 + pair], back_keep[0, 1, pair], back_other[0, 1, pair], back_x[1, pair])
        add_to(to_x.at[4 + pair], back_keep[1, 1, pair], back_other[1, 1, pair], back_y[1, pair])


def in_two_kernel(keep, other, by_x, by_y, first, second):
    for pair in range(2):
        add_to(first.at[pair], keep[0, 1, pair], other[0, 1, pair], by_x[2 + pair])
        add_to(second.at[pair], keep[1, 1, pair], other[1, 1, pair], by_y[2 + pair])


def in_plane_kernel(keep, other, by_x, by_y, by_xy, by_yx, near, kept):
    for q in range(TP):
        order, pair = q // 2, q % 2
        first, second = (by_x, by_xy) if order == 0 else (by_y, by_yx)
        out = near if q % 2 else kept
        add_to(out.at[q // 2], keep[order, 0, pair], other[order, 0, pair], first[pair], second[pair])


def back_plane_kernel(keep, other, by_x, by_y, mid_x, mid_y, near, kept):
    for q in range(TP):
        order, pair = q // 2, q % 2
        first, second = (by_x, mid_y) if order == 0 else (by_y, mid_x)
        out = near if q % 2 else kept
        add_to(out.at[q // 2], keep[order, 0, pair], other[order, 0, pair], first[0, pair], second[4 + pair])


def far_kernel(kept, near, far):
    add_to(far, kept[1], near[1])


def last_kernel(kept_a, near_a, far_a, kept_b, near_b, far_b, out):
    add_to(out.at[0], kept_a[0], near_a[0], far_a[...])
    add_to(out.at[1], kept_b[0], near_b[0], far_b[...])


def go_kernel(keep, other, own, send):
    add_to(own, keep[:, :GROUP_WIDTH], other[:, :GROUP_WIDTH])
    add_to(send, keep[:, GROUP_WIDTH:], other[:, GROUP_WIDTH:])


def near_kernel(keep, other, out):
    add_to(out, keep[QUARTER:], other[QUARTER:])


def tokens_kernel(keep, other, near, grad_in, out_here, tokens, again):
    add_to(tokens, keep[:QUARTER], other[:QUARTER], near[...], grad_in[...])
    again[...] = out_here[...]


TWO = 2 * SLICE


def qkv_two_kernel(la, ra, lb, rb, la_out, lb_out):
    add_to(la_out, la[TWO:], ra[TWO:])
    add_to(lb_out, lb[TWO:HELD], rb[TWO:HELD])


def qkv_three_kernel(la, ra, ra2, lb, rb, rb2, out):
    add_to(out.at[:TWO, :HALF], la[:TWO], ra[:TWO], ra2[:TWO])
    add_to(out.at[:TWO, HALF:], lb[:TWO], rb[:TWO], rb2[...])
    for n in range(2):
        rows = slice(HELD + n * VEC_ROWS, HELD + (n + 1) * VEC_ROWS)
        rows_two = slice(TWO + n * VEC_ROWS, TWO + (n + 1) * VEC_ROWS)
        add_to(out.at[TWO:, n * HALF : (n + 1) * HALF], la[rows], ra[rows], ra2[rows_two])


def qkv_four_kernel(own, other, out):
    add_to(out.at[:SLICE], own[:SLICE], other[SLICE:TWO])
    add_to(out.at[SLICE:TWO], own[SLICE:TWO], other[:SLICE])
    add_to(out.at[TWO:], own[TWO:], other[TWO:])


def mix_l_kernel(by_x, by_y, other, to_x, to_y):
    to_x[:TWO] = other[:TWO]
    to_x[TWO:] = by_y[SLICE:TWO]
    to_y[:TWO] = other[:TWO]
    to_y[TWO:] = by_x[:SLICE]


def diag_kernel(l_x, l_y, f_x, f_y, to_x, to_y):
    to_x[:SLICE] = l_y[SLICE:TWO]
    to_x[SLICE:] = f_y[1]
    to_y[:SLICE] = l_x[:SLICE]
    to_y[SLICE:] = f_x[0]


def plane_l_kernel(own, other, x_own, y_own, x_other, y_other, f_own, f_x, f_y, d_x, d_y, out):
    diag_own = (y_other[TWO:], x_other[TWO:])
    diag_other = (d_y[:SLICE], d_x[:SLICE])
    places = (
        ((own[:SLICE], own[SLICE:TWO]), (other[:SLICE], other[SLICE:TWO])),
        ((x_own[:SLICE], x_own[SLICE:TWO]), (x_other[:SLICE], x_other[SLICE:TWO])),
        ((y_own[:SLICE], y_own[SLICE:TWO]), (y_other[:SLICE], y_other[SLICE:TWO])),
        (diag_own, diag_other),
    )
    for p, (here, there) in enumerate(places):
        for slot in range(TP):
            at = (p * TP + slot) * SLICE
            out[at : at + SLICE] = (there if slot % 2 else here)[slot // 2]
    add_to(out.at[16 * SLICE : FFN_AT], own[TWO:], other[TWO:])
    for n, (left, right) in enumerate(
        ((f_own[0], f_own[1]), (f_x[0], f_x[1]), (f_y[0], f_y[1]), (d_y[SLICE:], d_x[SLICE:]))
    ):
        out[FFN_AT + 2 * n * SLICE : FFN_AT + (2 * n + 1) * SLICE] = left
        out[FFN_AT + (2 * n + 1) * SLICE : FFN_AT + (2 * n + 2) * SLICE] = right


VMEM = pl.BlockSpec(memory_space=pltpu.VMEM)
SMEM = pl.BlockSpec(memory_space=pltpu.SMEM)
HBM = pl.BlockSpec(memory_space=pl.ANY)


def call(kernel, in_specs, outs, scratch, vmem_mib, name, deps=()):
    count, extra = len(in_specs), len(deps)

    def body(*refs):
        kernel(*refs[:count], *refs[count + extra :])

    run = pl.pallas_call(
        body,
        out_shape=[jax.ShapeDtypeStruct(shape, dtype) for shape, dtype in outs],
        in_specs=list(in_specs) + [HBM] * extra,
        out_specs=[VMEM] * len(outs),
        scratch_shapes=scratch,
        compiler_params=pltpu.CompilerParams(vmem_limit_bytes=vmem_mib * 1024 * 1024),
        cost_estimate=pl.CostEstimate(flops=1, bytes_accessed=1, transcendentals=0),
        name=name,
    )
    return lambda *arrays: run(*arrays, *deps)


def step(kernel, name, outs, *arrays, deps=()):
    shapes = [(shape, bf16) for shape in outs]
    result = call(kernel, [VMEM] * len(arrays), shapes, [], 12, name, deps)(*arrays)
    return result[0] if len(outs) == 1 else result


def per_device(
    tokens,
    w_qkv,
    bias_query,
    bias_value,
    w_out,
    bias_out,
    gain_attn,
    shift_attn,
    w_in,
    bias_in,
    w_back,
    bias_back,
    gain_ffn,
    shift_ffn,
    random_blocks,
    cotangent,
):
    dp_count = lax.axis_size("dp")
    d = lax.axis_index("dp")
    z = lax.axis_index("tp")
    core = d & 1
    quarter = (z & 1) + 2 * core
    mine = d & (SLOTS - 1)
    here = ((d >> 1) & 1) * 4 + ((d >> 2) & 1) * 2 + (z >> 1)
    native = (core == z // 2).astype(jnp.int32)
    info = jnp.stack([quarter, mine, z, here, native]).astype(jnp.int32)
    extra_bits = [1 << b for b in range(3, dp_count.bit_length() - 1)]

    own_tokens = place(tokens[0])
    piece = call(
        piece_kernel,
        [SMEM, HBM, VMEM, VMEM],
        [((2 * SLICE + VEC_ROWS, WIDTH), bf16)],
        [pltpu.VMEM((WIDTH, WIDTH), bf16), pltpu.SemaphoreType.DMA],
        8,
        "piece",
    )(info, w_in, w_back, bias_in)[0]
    piece_one = hop(piece, 0, 1)
    piece_two = hop(piece, 0, 2)
    random_own = random_blocks.reshape(-1)
    random_other = hop(random_own, CORE, 0)
    w_group, bias_group = call(
        group_kernel,
        [SMEM, VMEM, VMEM, VMEM],
        [((WIDTH, 3 * GROUP_WIDTH), bf16), ((1, 3 * GROUP_WIDTH), f32)],
        [],
        16,
        "group",
    )(info, w_qkv, bias_query, bias_value)
    near_tokens = hop(own_tokens, 0, 1)
    core_tokens = hop(own_tokens, CORE, 0)
    far_tokens = hop(near_tokens, CORE, 0)
    part_one = step(
        join_kernel, "pair", [(2 * PIECE, WIDTH)], piece_one, piece_two, deps=(own_tokens, w_group, random_other)
    )
    x_one = hop(part_one, X_BIT, 0)
    y_one = hop(part_one, Y_BIT, 0)
    piece_three = hop(piece_two, 0, 1)
    cot = place(cotangent[0])
    to_x, to_y = step(
        mix_kernel,
        "mix",
        [(3 * PIECE - 2 * CUT, WIDTH), (PIECE + 2 * CUT, WIDTH)],
        x_one,
        y_one,
        piece_three,
        deps=(near_tokens,),
    )
    x_three = hop(to_x, X_BIT, 0)
    y_three = hop(to_y, Y_BIT, 0)

    packed = ((PACKED, 2 * HEAD_DIM), bf16)
    double = ((2 * PACKED, 2 * HEAD_DIM), bf16)
    per_head = ((LENGTH, HEAD_DIM), bf16)
    token_slots = (own_tokens, near_tokens, core_tokens, far_tokens)
    a0, a13, a2, *heads = call(
        attention_kernel,
        [SMEM] * 3 + [VMEM] * 6,
        [packed, double, packed] + [per_head] * 9 + [((16, QUARTER), f32)],
        [pltpu.VMEM((GROUP, LENGTH, HEAD_DIM), bf16)],
        24,
        "attention",
        (to_x, core_tokens),
    )(info, random_own, random_other, *token_slots, w_group, bias_group)
    heads, lse = heads[:9], heads[9]
    a1 = hop(a13, 0, 1)
    a2 = hop(a2, CORE, 0)
    a3 = hop(a1[PACKED:], CORE, 0)
    to_x, to_y = step(
        last_mix_kernel,
        "mix_last",
        [(PIECE - CUT, WIDTH), (CUT, WIDTH)],
        x_three,
        y_three,
        deps=(a0, cot),
    )
    last_back = hop(to_x, X_BIT, 0)
    last_in = hop(to_y, Y_BIT, 0)
    held = step(
        held_kernel,
        "held",
        [(11 * PIECE, WIDTH)],
        part_one,
        x_one,
        y_one,
        piece_three,
        x_three,
        y_three,
        deps=(a2, cot),
    )
    tokens_t = call(flip_kernel, [VMEM] * 4, [((WIDTH, LENGTH), bf16)], [], 8, "flip_tokens", (a1, held))(
        *token_slots
    )[0]
    last = step(join_kernel, "last_piece", [(PIECE, WIDTH)], last_in, last_back, deps=(tokens_t,))
    quarters = ((TP - 1, WIDTH, WIDTH), bf16)
    w_in_s, w_back_s, w_out_s, bias_s = call(
        assemble_kernel,
        [SMEM] + [VMEM] * 6,
        [quarters, quarters, ((WIDTH, WIDTH), bf16), ((TP - 1, VEC_ROWS, WIDTH), bf16)],
        [],
        20,
        "assemble",
    )(info, held, hop(held, CORE, 0), last_in, last_back, hop(last, CORE, 0), w_out)

    rows = ((QUARTER, WIDTH), bf16)
    wide = ((QUARTER, TP * WIDTH), bf16)
    rows_f32 = ((QUARTER, WIDTH), f32)
    vec_rows = ((VEC_ROWS, WIDTH), f32)
    out_here, first_in, grad_second, ffn_input, grad_branch, activated, gelu_slope, attended, vectors = call(
        ffn_kernel,
        [SMEM] + [VMEM] * 19,
        [rows, rows_f32, rows_f32, rows, rows, wide, ((QUARTER, TP * WIDTH), f32), rows, vec_rows],
        [],
        20,
        "ffn",
        (tokens_t,),
    )(
        info,
        own_tokens,
        a0,
        a1,
        a2,
        a3,
        bias_out,
        gain_attn,
        shift_attn,
        bias_back,
        gain_ffn,
        shift_ffn,
        bias_in,
        cot,
        w_out_s,
        w_in,
        w_back,
        w_in_s,
        w_back_s,
        bias_s,
    )
    pairs = ((2, SLOTS // 2, 2, SLICE, WIDTH), bf16)
    halves = ((WIDTH, 2 * GROUP_WIDTH), bf16)
    flips = [pltpu.VMEM((WIDTH, QUARTER), bf16), pltpu.VMEM((WIDTH, QUARTER), bf16)]
    back_keep, back_send = call(
        weight_grads, [SMEM] + [VMEM] * 2, [pairs] * 2, flips, 12, "back_grads"
    )(info, grad_branch, activated)
    back_other = hop(back_send, CORE, 0)

    g0, g13, g2, grad_in, vectors, in_keep, in_send, go_keep, go_send = call(
        ffn_back_kernel,
        [SMEM] + [VMEM] * 13,
        [packed, double, packed, rows_f32, vec_rows] + [pairs] * 2 + [halves] * 2,
        [pltpu.VMEM((QUARTER, TP * WIDTH), bf16)] + flips,
        20,
        "ffn_back",
        (back_keep,),
    )(
        info,
        first_in,
        grad_second,
        grad_branch,
        gelu_slope,
        gain_attn,
        vectors,
        w_out_s,
        w_in,
        w_back,
        w_in_s,
        w_back_s,
        ffn_input,
        attended,
    )
    g1 = hop(g13, 0, 1)
    g2 = hop(g2, CORE, 0)
    g3 = hop(g1[PACKED:], CORE, 0)

    first_level = [(2, 2, SLICE, WIDTH)] * 2
    def hop_pair(pair, first, second):
        return hop(pair[0], first, 0), hop(pair[1], second, 0)

    back_sums = step(level_one_kernel, "back_one", first_level, back_keep, back_other, deps=(g13,))
    back_x, back_y = hop_pair(back_sums, X_BIT, Y_BIT)
    in_other = hop(in_send, CORE, 0)
    go_other = hop(go_send, CORE, 0)

    def head_back(h, deps):
        return call(
            functools.partial(attention_back_kernel, h),
            [SMEM] * 3 + [VMEM] * 8,
            [((LENGTH, 3 * HEAD_DIM), bf16), ((8, 3 * HEAD_DIM), f32)],
            [
                pltpu.VMEM((LENGTH, HEAD_DIM), bf16),
                pltpu.VMEM((LENGTH, HEAD_DIM), f32),
                pltpu.VMEM((LENGTH, HEAD_DIM), f32),
                pltpu.VMEM((LENGTH, HEAD_DIM), f32),
            ],
            12,
            f"attention_back_{h}",
            deps,
        )(info, random_own, random_other, *heads[3 * h : 3 * h + 3], lse, g0, g1, g2, g3)

    go_own, go_send = step(go_kernel, "go", [(WIDTH, GROUP_WIDTH)] * 2, go_keep, go_other)
    go_near = hop(go_send, 0, 1)
    gh0, s0 = head_back(0, (go_own, back_sums[0]))
    back_parts = [back_keep, back_other, back_x, back_y]
    to_x, to_y = step(
        middle_kernel,
        "middle",
        [(6, SLICE, WIDTH)] * 2,
        in_keep,
        in_other,
        *back_parts,
        deps=(gh0,),
    )
    mid_x, mid_y = hop(to_x, X_BIT, 0), hop(to_y, Y_BIT, 0)
    in_parts = [in_keep, in_other, mid_x, mid_y]
    z_level = [(2, SLICE, WIDTH)] * 2
    gh1, s1 = head_back(1, (to_x,))
    gh2, s2 = head_back(2, (gh1,))

    la_keep, la_send, lb_keep, lb_send = call(
        qkv_grad_kernel,
        [SMEM] + [VMEM] * 10,
        [((HELD + 2 * VEC_ROWS, HALF), bf16)] * 4,
        [pltpu.VMEM((WIDTH, 4 * GROUP_WIDTH), bf16)],
        16,
        "qkv_grads",
        (gh2,),
    )(info, tokens_t, gh0, gh1, gh2, go_own, go_near, vectors, s0, s1, s2)
    ra = hop(la_send, X_BIT, 0)
    rb = hop(lb_send, Y_BIT, 0)

    keep, send = call(
        token_grad_kernel,
        [VMEM] * 4,
        [((LENGTH // 2, WIDTH), bf16)] * 2,
        [pltpu.VMEM((LENGTH, 3 * GROUP_WIDTH), bf16)],
        16,
        "token_grad",
        (la_keep,),
    )(gh0, gh1, gh2, w_group)
    other = hop(send, CORE, 0)
    near_b, kept_b = step(
        back_plane_kernel, "back_plane", z_level, *back_parts, mid_x, mid_y, deps=(keep,)
    )
    near_b = hop(near_b, 0, 1)
    sums = step(in_two_kernel, "in_two", z_level, *in_parts, deps=(kept_b,))
    in_parts += hop_pair(sums, Y_BIT, X_BIT)
    near_low = step(near_kernel, "near", [(QUARTER, WIDTH)], keep, other, deps=(sums[0],))
    near = hop(near_low, 0, 1)
    far_b = step(far_kernel, "far_back", [(SLICE, WIDTH)], kept_b, near_b, deps=(near_low,))
    far_hop_b = hop(far_b, 0, 2)
    la2, lb2 = step(
        qkv_two_kernel,
        "qkv_two",
        [(TWO + 2 * VEC_ROWS, HALF), (TWO, HALF)],
        la_keep,
        ra,
        lb_keep,
        rb,
        deps=(far_b,),
    )
    ra2 = hop(la2, Y_BIT, 0)
    rb2 = hop(lb2, X_BIT, 0)
    rows_l = (TWO + VEC_ROWS, WIDTH)
    near_a, kept_a = step(in_plane_kernel, "in_plane", z_level, *in_parts, deps=(la2,))
    near_a = hop(near_a, 0, 1)
    partial = step(
        qkv_three_kernel, "qkv_three", [rows_l], la_keep, ra, ra2, lb_keep, rb, rb2, deps=(kept_a, far_hop_b)
    )
    far_a = step(far_kernel, "far_in", [(SLICE, WIDTH)], kept_a, near_a, deps=(partial, far_hop_b))
    far_hop_a = hop(far_a, 0, 2)
    sum_l = step(
        qkv_four_kernel, "qkv_four", [rows_l], partial, hop(partial, 0, 2), deps=(far_a, near)
    )
    for bit in extra_bits:
        sum_l = add_low(sum_l, hop(sum_l, bit, 0))

    own_l = sum_l[:TWO]
    x_own = hop(own_l, X_BIT, 0)
    y_own = hop(own_l, Y_BIT, 0)
    other_l = hop(sum_l, 0, 1)
    to_x, to_y = step(
        mix_l_kernel, "mix_l", [(TWO + SLICE, WIDTH)] * 2, x_own, y_own, other_l
    )
    x_other = hop(to_x, X_BIT, 0)
    y_other = hop(to_y, Y_BIT, 0)
    sum_f = step(
        last_kernel,
        "last",
        [(2, SLICE, WIDTH)],
        kept_a,
        near_a,
        far_hop_a,
        kept_b,
        near_b,
        far_hop_b,
        deps=(to_x,),
    )
    for bit in extra_bits:
        sum_f = add_low(sum_f, hop(sum_f, bit, 0))
    low_outs = step(
        tokens_kernel,
        "tokens",
        [(QUARTER, WIDTH)] * 2,
        keep,
        other,
        near,
        grad_in,
        out_here,
        deps=(sum_f,),
    )
    token_grads, layer_out = place(low_outs[0]), place(low_outs[1])
    f_x = hop(sum_f, X_BIT, 0)
    f_y = hop(sum_f, Y_BIT, 0)
    diag = step(diag_kernel, "diag", [(TWO, WIDTH)] * 2, x_other, y_other, f_x, f_y)
    d_x, d_y = hop_pair(diag, X_BIT, Y_BIT)
    plane = step(
        plane_l_kernel,
        "plane",
        [(FFN_AT + SLOTS * SLICE, WIDTH)],
        sum_l,
        other_l,
        x_own,
        y_own,
        x_other,
        y_other,
        sum_f,
        f_x,
        f_y,
        d_x,
        d_y,
        deps=(token_grads, layer_out),
    )
    square = ((WIDTH, WIDTH), f32)
    halves_out = [((WIDTH, 3 * WIDTH), f32), square, square]
    half_scratch = [
        pltpu.VMEM((WIDTH, 3 * HALF_GROUPS), f32),
        pltpu.VMEM((HALF_GROUPS, WIDTH), f32),
        pltpu.VMEM((WIDTH // 2, WIDTH), f32),
        pltpu.SemaphoreType.DMA((2 * SLOTS + 1,)),
    ]
    as_shape = lambda outs: [jax.ShapeDtypeStruct(shape, dtype) for shape, dtype in outs]
    cheap = pl.CostEstimate(flops=1, bytes_accessed=1, transcendentals=0)
    *half_written, layer_out, grad_tokens = pl.pallas_call(
        first_half_kernel,
        out_shape=as_shape(halves_out + [rows, rows]),
        in_specs=[SMEM] + [VMEM] * 3,
        out_specs=[HBM] * 5,
        scratch_shapes=half_scratch + [pltpu.SemaphoreType.DMA((2,))],
        compiler_params=pltpu.CompilerParams(vmem_limit_bytes=16 * 1024 * 1024),
        cost_estimate=cheap,
        name="first_half",
    )(info, plane, token_grads, layer_out)
    grad_w_qkv, grad_w_out, grad_w_in, grad_w_back, *vec_outs = pl.pallas_call(
        second_half_kernel,
        out_shape=as_shape(halves_out + [square] + [((WIDTH,), f32)] * 9),
        in_specs=[SMEM, VMEM, VMEM] + [HBM] * 3,
        out_specs=[HBM] * 4 + [VMEM] * 9,
        scratch_shapes=half_scratch + [pltpu.VMEM((WIDTH, WIDTH), f32)] * 2 + [pltpu.SemaphoreType.DMA],
        input_output_aliases={3: 0, 4: 1, 5: 2},
        compiler_params=pltpu.CompilerParams(vmem_limit_bytes=24 * 1024 * 1024),
        cost_estimate=cheap,
        name="second_half",
    )(info, plane, hop(plane, CORE, 0), *half_written)
    (
        grad_shift_ffn,
        grad_gain_ffn,
        grad_bias_back,
        grad_shift_attn,
        grad_gain_attn,
        grad_bias_out,
        grad_bias_query,
        grad_bias_value,
        grad_bias_in,
    ) = vec_outs
    return (
        layer_out[None],
        grad_tokens[None],
        grad_w_qkv,
        grad_bias_query,
        grad_bias_value,
        grad_w_out,
        grad_bias_out,
        grad_gain_attn,
        grad_shift_attn,
        grad_w_in,
        grad_bias_in,
        grad_w_back,
        grad_bias_back,
        grad_gain_ffn,
        grad_shift_ffn,
    )


def solution(mesh):
    in_specs = (
        P("dp", "tp", None),
        P(),
        P(),
        P(),
        P(),
        P(),
        P(),
        P(),
        P(None, "tp"),
        P("tp"),
        P("tp", None),
        P(),
        P(),
        P(),
        P("dp", None, None, None),
        P("dp", "tp", None),
    )
    out_specs = (
        P("dp", "tp", None),
        P("dp", "tp", None),
        P(),
        P(),
        P(),
        P(),
        P(),
        P(),
        P(),
        P(None, "tp"),
        P("tp"),
        P("tp", None),
        P(),
        P(),
        P(),
    )
    return jax.shard_map(
        per_device, mesh=mesh, in_specs=in_specs, out_specs=out_specs, check_vma=False
    )
```

profile of v0, /device:TPU:1, one launch (start us, length us, event | category | flops | bytes accessed | tf_op | source)
XLA Modules:
  0.0 217.5 jit_solution(2838057222865183048)
XLA Ops:
  0.7 5.7 %collective-permute-start = (bf16[256,768]{1,0:T(8,128)(2,1)}, bf16[256,768]{1,0:T(8,128)(2,1)S(1)}, u32[]{:S(2)}, u32[]{:S(2)}) collective-permute-start(bf16[256,768]{1,0:T(8,128)(2,1)} %bitcast.11), channel_id=1, source_target_pairs={{0,0},{1,1},{2,4},{3,5},{4,2},{5,3},{6,6},{7,7},{8,8},{9,9},{10,12... | collective-permute-start | bytes 1179656 | tf_op jit(solution)/shard_map/ppermute | solution.py:67
  6.5 1.3 copy-done
  7.8 1.3 copy-done.2
  11.0 1.4 collective-permute-start.5
  13.3 2.0 copy-done.4
  16.2 11.1 %collective-permute-done.6.refs_1_ = bf16[208,768]{1,0:T(8,128)(2,1)S(1)} collective-permute-done((bf16[208,768]{1,0:T(8,128)(2,1)S(1)}, bf16[208,768]{1,0:T(8,128)(2,1)S(1)}, u32[]{:S(2)}, u32[]{:S(2)}) %collective-permute-start.6) | collective-permute-done | bytes 319520 | tf_op jit(solution)/shard_map/ppermute | solution.py:56
  27.4 1.3 collective-permute-start.8
  28.7 1.2 collective-permute-start.7
  29.9 3.1 %collective-permute-start.1 = (bf16[256,768]{1,0:T(8,128)(2,1)S(1)}, bf16[256,768]{1,0:T(8,128)(2,1)S(1)}, u32[]{:S(2)}, u32[]{:S(2)}) collective-permute-start(bf16[256,768]{1,0:T(8,128)(2,1)S(1)} %collective-permute-done.refs_2_.refs_3_.refs_0_.refs_1_), channel_id=1, source_target_pairs={{0,1},{1,0},{2,3},{3,2},{4,5},{5,4},{6,7},{7,6},{8,9},{9,8},{10,11... | collective-permute-start | bytes 1179656 | tf_op jit(solution)/shard_map/ppermute | solution.py:56
  33.0 14.5 %collective-permute-done.9.refs_2_.refs_3_ = bf16[208,768]{1,0:T(8,128)(2,1)S(1)} collective-permute-done((bf16[208,768]{1,0:T(8,128)(2,1)S(1)}, bf16[208,768]{1,0:T(8,128)(2,1)S(1)}, u32[]{:S(2)}, u32[]{:S(2)}) %collective-permute-start.9) | collective-permute-done | bytes 319520 | tf_op jit(solution)/shard_map/ppermute | solution.py:56
  48.2 2.9 %collective-permute-start.2 = (bf16[256,768]{1,0:T(8,128)(2,1)S(1)}, bf16[256,768]{1,0:T(8,128)(2,1)S(1)}, u32[]{:S(2)}, u32[]{:S(2)}) collective-permute-start(bf16[256,768]{1,0:T(8,128)(2,1)S(1)} %collective-permute-done.refs_2_.refs_3_.refs_0_.refs_1_), channel_id=1, source_target_pairs={{0,4},{1,5},{2,6},{3,7},{4,0},{5,1},{6,2},{7,3},{8,12},{9,13},{10,... | collective-permute-start | bytes 1179656 | tf_op jit(solution)/shard_map/ppermute | solution.py:56
  51.1 3.8 %collective-permute-start.14 = (bf16[256,768]{1,0:T(8,128)(2,1)S(1)}, bf16[256,768]{1,0:T(8,128)(2,1)S(1)}, u32[]{:S(2)}, u32[]{:S(2)}) collective-permute-start(bf16[256,768]{1,0:T(8,128)(2,1)S(1)} %bitcast.12), channel_id=1, source_target_pairs={{0,0},{1,1},{2,4},{3,5},{4,2},{5,3},{6,6},{7,7},{8,8},{9,9},{10,12... | collective-permute-start | bytes 1179656 | tf_op jit(solution)/shard_map/ppermute | solution.py:67
  54.9 9.9 %attention.1 = (bf16[384,128]{1,0:T(8,128)(2,1)S(1)}, bf16[768,128]{1,0:T(8,128)(2,1)S(1)}, bf16[384,128]{1,0:T(8,128)(2,1)S(1)}, bf16[1024,64]{1,0:T(8,128)(2,1...) custom-call(s32[5]{0:T(128)S(1)} %stack.27.refs_0_.info, ...), custom_call_target="tpu_custom_call" | custom-call | flops 1 | bytes 1 | tf_op jit(solution)/shard_map/attention/pallas_call | solution.py:692
  69.3 3.6 %collective-permute-done.10.refs_4_.refs_3_ = bf16[768,128]{1,0:T(8,128)(2,1)S(1)} collective-permute-done((bf16[768,128]{1,0:T(8,128)(2,1)S(1)}, bf16[768,128]{1,0:T(8,128)(2,1)S(1)}, u32[]{:S(2)}, u32[]{:S(2)}) %collective-permute-start.10) | collective-permute-done | bytes 196640 | tf_op jit(solution)/shard_map/ppermute | solution.py:56
  73.4 1.2 collective-permute-start.19
  77.1 5.8 %ffn.1 = (bf16[256,768]{1,0:T(8,128)(2,1)S(1)}, f32[256,768]{1,0:T(8,128)S(1)}, f32[256,768]{1,0:T(8,128)S(1)}, bf16[256,768]{1,0:T(8,128)(2,1)S(1)}, bf16[256,7...) custom-call(s32[5]{0:T(128)S(1)} %stack.27.refs_0_.info, ...), custom_call_target="tpu_custom_call" | custom-call | flops 1 | bytes 1 | tf_op jit(solution)/shard_map/ffn/pallas_call | solution.py:692
  82.9 2.0 back_grads.1
  85.4 5.6 %ffn_back.1 = (bf16[384,128]{1,0:T(8,128)(2,1)S(1)}, bf16[768,128]{1,0:T(8,128)(2,1)S(1)}, bf16[384,128]{1,0:T(8,128)(2,1)S(1)}, f32[256,768]{1,0:T(8,128)S(1)},...) custom-call(s32[5]{0:T(128)S(1)} %stack.27.refs_0_.info, ...), custom_call_target="tpu_custom_call" | custom-call | flops 1 | bytes 1 | tf_op jit(solution)/shard_map/ffn_back/pallas_call | solution.py:692
  91.9 1.3 collective-permute-start.27
  93.2 1.2 collective-permute-start.26
  94.9 5.2 %collective-permute-done.20.refs_8_ = bf16[768,128]{1,0:T(8,128)(2,1)S(1)} collective-permute-done((bf16[768,128]{1,0:T(8,128)(2,1)S(1)}, bf16[768,128]{1,0:T(8,128)(2,1)S(1)}, u32[]{:S(2)}, u32[]{:S(2)}) %collective-permute-start.20) | collective-permute-done | bytes 196640 | tf_op jit(solution)/shard_map/ppermute | solution.py:56
  100.1 1.6 collective-permute-start.21
  103.2 4.9 %attention_back_0.1 = (bf16[1024,192]{1,0:T(8,128)(2,1)S(1)}, f32[8,192]{1,0:T(8,128)S(1)}) custom-call(s32[5]{0:T(128)S(1)} %stack.27.refs_0_.info, s32[576]{0:T(1024)S(1)} %reshape.33.refs_1_, s32[576]{0:T(1024)S(1)} %collective-permute-done.4.refs_4_.refs_2_, bf16[1024,64]{1,0:T(8,128)(2,1)S(1)} %get-tuple-element.114.refs_3_, ...), custom_call_target="tpu_custom_call" | custom-call | flops 1 | bytes 1 | tf_op jit(solution)/shard_map/attention_back_0/pallas_call | solution.py:692
  109.8 4.5 %attention_back_1.1 = (bf16[1024,192]{1,0:T(8,128)(2,1)S(1)}, f32[8,192]{1,0:T(8,128)S(1)}) custom-call(s32[5]{0:T(128)S(1)} %stack.27.refs_0_.info, s32[576]{0:T(1024)S(1)} %reshape.33.refs_1_, s32[576]{0:T(1024)S(1)} %collective-permute-done.4.refs_4_.refs_2_, bf16[1024,64]{1,0:T(8,128)(2,1)S(1)} %get-tuple-element.143.refs_3_, ...), custom_call_target="tpu_custom_call" | custom-call | flops 1 | bytes 1 | tf_op jit(solution)/shard_map/attention_back_1/pallas_call | solution.py:692
  114.4 4.5 %attention_back_2.1 = (bf16[1024,192]{1,0:T(8,128)(2,1)S(1)}, f32[8,192]{1,0:T(8,128)S(1)}) custom-call(s32[5]{0:T(128)S(1)} %stack.27.refs_0_.info, s32[576]{0:T(1024)S(1)} %reshape.33.refs_1_, s32[576]{0:T(1024)S(1)} %collective-permute-done.4.refs_4_.refs_2_, bf16[1024,64]{1,0:T(8,128)(2,1)S(1)} %get-tuple-element.151.refs_3_, ...), custom_call_target="tpu_custom_call" | custom-call | flops 1 | bytes 1 | tf_op jit(solution)/shard_map/attention_back_2/pallas_call | solution.py:692
  118.9 2.1 qkv_grads.1
  121.0 1.5 token_grad.1
  122.5 1.7 collective-permute-start.34
  124.6 1.2 collective-permute-start.30
  125.8 3.2 %collective-permute-done.32.refs_5_.refs_3_ = bf16[6,96,768]{2,1,0:T(8,128)(2,1)S(1)} collective-permute-done((bf16[6,96,768]{2,1,0:T(8,128)(2,1)S(1)}, bf16[6,96,768]{2,1,0:T(8,128)(2,1)S(1)}, u32[]{:S(2)}, u32[]{:S(2)}) %collective-permute-start.32) | collective-permute-done | bytes 884768 | tf_op jit(solution)/shard_map/ppermute | solution.py:56
  132.0 3.2 %collective-permute-done.33.refs_1_.refs_4_ = bf16[2,96,768]{2,1,0:T(8,128)(2,1)S(1)} collective-permute-done((bf16[2,96,768]{2,1,0:T(8,128)(2,1)S(1)}, bf16[2,96,768]{2,1,0:T(8,128)(2,1)S(1)}, u32[]{:S(2)}, u32[]{:S(2)}) %collective-permute-start.33) | collective-permute-done | bytes 294944 | tf_op jit(solution)/shard_map/ppermute | solution.py:56
  135.9 1.2 collective-permute-start.35
  137.1 1.6 collective-permute-start.39
  139.0 3.0 %collective-permute-done.38.refs_5_ = bf16[2,96,768]{2,1,0:T(8,128)(2,1)S(1)} collective-permute-done((bf16[2,96,768]{2,1,0:T(8,128)(2,1)S(1)}, bf16[2,96,768]{2,1,0:T(8,128)(2,1)S(1)}, u32[]{:S(2)}, u32[]{:S(2)}) %collective-permute-start.38) | collective-permute-done | bytes 294944 | tf_op jit(solution)/shard_map/ppermute | solution.py:56
  143.6 1.6 collective-permute-done.36.refs_5_
  145.6 1.7 collective-permute-start.40
  147.8 17.6 %collective-permute-done.41.refs_1_ = bf16[2,96,768]{2,1,0:T(8,128)(2,1)S(1)} collective-permute-done((bf16[2,96,768]{2,1,0:T(8,128)(2,1)S(1)}, bf16[2,96,768]{2,1,0:T(8,128)(2,1)S(1)}, u32[]{:S(2)}, u32[]{:S(2)}) %collective-permute-start.41) | collective-permute-done | bytes 294944 | tf_op jit(solution)/shard_map/ppermute | solution.py:56
  165.6 1.9 collective-permute-start.45
  167.6 2.0 collective-permute-start.48
  169.6 1.9 collective-permute-done.45.refs_1_.refs_3_
  171.5 1.8 collective-permute-done.44.refs_0_.refs_2_
  177.0 9.9 %collective-permute-start.53 = (bf16[256,768]{1,0:T(8,128)(2,1)S(1)}, bf16[256,768]{1,0:T(8,128)(2,1)S(1)}, u32[]{:S(2)}, u32[]{:S(2)}) collective-permute-start(bf16[256,768]{1,0:T(8,128)(2,1)S(1)} %get-tuple-element.181), channel_id=1, source_target_pairs={{0,0},{1,1},{2,4},{3,5},{4,2},{5,3},{6,6},{7,7},{8,8},{9,9},{10,12... | collective-permute-start | bytes 1179656 | tf_op jit(solution)/shard_map/ppermute | solution.py:67
  186.9 9.3 %collective-permute-start.54 = (bf16[256,768]{1,0:T(8,128)(2,1)S(1)}, bf16[256,768]{1,0:T(8,128)(2,1)S(1)}, u32[]{:S(2)}, u32[]{:S(2)}) collective-permute-start(bf16[256,768]{1,0:T(8,128)(2,1)S(1)} %get-tuple-element.182), channel_id=1, source_target_pairs={{0,0},{1,1},{2,4},{3,5},{4,2},{5,3},{6,6},{7,7},{8,8},{9,9},{10,12... | collective-permute-start | bytes 1179656 | tf_op jit(solution)/shard_map/ppermute | solution.py:67
  196.7 1.3 collective-permute-start.52
  198.0 7.9 %collective-permute-done.54.refs_12_.low_out = bf16[256,768]{1,0:T(8,128)(2,1)S(1)} collective-permute-done((bf16[256,768]{1,0:T(8,128)(2,1)S(1)}, bf16[256,768]{1,0:T(8,128)(2,1)S(1)}, u32[]{:S(2)}, u32[]{:S(2)}) %collective-permute-start.54) | collective-permute-done | bytes 393248 | tf_op jit(solution)/shard_map/ppermute | solution.py:67
  206.2 3.6 %first_half.1 = (f32[768,2304]{1,0:T(8,128)}, f32[768,768]{1,0:T(8,128)}, f32[768,768]{1,0:T(8,128)}, bf16[256,768]{1,0:T(8,128)(2,1)}, bf16[256,768]{1,0:T(8,128)(2,1)}) custom-call(s32[5]{0:T(128)S(1)} %stack.27.refs_0_.info, bf16[2320,768]{1,0:T(8,128)(2,1)S(1)} %plane.1, bf16[256,768]{1,0:T(8,128)(2,1)S(1)} %collective-permute-done.53.refs_11_.low_tokens, ...), custom_call_target="tpu_custom_call" | custom-call | flops 1 | bytes 1 | tf_op jit(solution)/shard_map/first_half/pallas_call | solution.py:1064
  209.8 2.6 %collective-permute-done.55.other = bf16[2320,768]{1,0:T(8,128)(2,1)S(1)} collective-permute-done((bf16[2320,768]{1,0:T(8,128)(2,1)S(1)}, bf16[2320,768]{1,0:T(8,128)(2,1)S(1)}, u32[]{:S(2)}, u32[]{:S(2)}) %collective-permute-start.55) | collective-permute-done | bytes 3563552 | tf_op jit(solution)/shard_map/ppermute | solution.py:56
  212.4 4.9 %second_half.1 = (f32[768,2304]{1,0:T(8,128)}, f32[768,768]{1,0:T(8,128)}, f32[768,768]{1,0:T(8,128)}, f32[768,768]{1,0:T(8,128)}, f32[768]{0:T(1024)}, /*index=...) custom-call(s32[5]{0:T(128)S(1)} %stack.27.refs_0_.info, ...), custom_call_target="tpu_custom_call", output_to_operand_aliasing={{0}: (3, {}), {1}: (4, {}), {2}: (5, {})} | custom-call | flops 1 | bytes 1 | tf_op jit(solution)/shard_map/second_half/pallas_call | solution.py:1074
  (143 shorter events, 28.3 us)
Async XLA Ops:
  0.7 26.7 %collective-permute-start = (bf16[256,768]{1,0:T(8,128)(2,1)}, bf16[256,768]{1,0:T(8,128)(2,1)S(1)}, u32[]{:S(2)}, u32[]{:S(2)}) collective-permute-start(bf16[256,768]{1,0:T(8,128)(2,1)} %bitcast.11), channel_id=1, source_target_pairs={{0,0},{1,1},{2,4},{3,5},{4,2},{5,3},{6,6},{7,7},{8,8},{9,9},{10,12... | collective-permute-start | bytes 1179656 | tf_op jit(solution)/shard_map/ppermute | solution.py:67
  10.9 16.5 %collective-permute-start.6 = (bf16[208,768]{1,0:T(8,128)(2,1)S(1)}, bf16[208,768]{1,0:T(8,128)(2,1)S(1)}, u32[]{:S(2)}, u32[]{:S(2)}) collective-permute-start(bf16[208,768]{1,0:T(8,128)(2,1)S(1)} %piece.1), channel_id=1, source_target_pairs={{0,2},{1,3},{2,0},{3,1},{4,6},{5,7},{6,4},{7,5},{8,10},{9,11},{10,... | collective-permute-start | bytes 958472 | tf_op jit(solution)/shard_map/ppermute | solution.py:56
  11.0 16.4 %collective-permute-start.5 = (bf16[208,768]{1,0:T(8,128)(2,1)S(1)}, bf16[208,768]{1,0:T(8,128)(2,1)S(1)}, u32[]{:S(2)}, u32[]{:S(2)}) collective-permute-start(bf16[208,768]{1,0:T(8,128)(2,1)S(1)} %piece.1), channel_id=1, source_target_pairs={{0,1},{1,0},{2,3},{3,2},{4,5},{5,4},{6,7},{7,6},{8,9},{9,8},{10,11... | collective-permute-start | bytes 958472 | tf_op jit(solution)/shard_map/ppermute | solution.py:56
  27.4 20.2 %collective-permute-start.8 = (bf16[416,768]{1,0:T(8,128)(2,1)S(1)}, bf16[416,768]{1,0:T(8,128)(2,1)S(1)}, u32[]{:S(2)}, u32[]{:S(2)}) collective-permute-start(bf16[416,768]{1,0:T(8,128)(2,1)S(1)} %pair.1.refs_0_), channel_id=1, source_target_pairs={{0,16},{1,17},{2,18},{3,19},{4,20},{5,21},{6,22},{7,23},{8,24},{9,... | collective-permute-start | bytes 1916936 | tf_op jit(solution)/shard_map/ppermute | solution.py:56
  28.7 18.9 %collective-permute-start.7 = (bf16[416,768]{1,0:T(8,128)(2,1)S(1)}, bf16[416,768]{1,0:T(8,128)(2,1)S(1)}, u32[]{:S(2)}, u32[]{:S(2)}) collective-permute-start(bf16[416,768]{1,0:T(8,128)(2,1)S(1)} %pair.1.refs_0_), channel_id=1, source_target_pairs={{0,8},{1,9},{2,10},{3,11},{4,12},{5,13},{6,14},{7,15},{8,0},{9,1},... | collective-permute-start | bytes 1916936 | tf_op jit(solution)/shard_map/ppermute | solution.py:56
  29.9 17.7 %collective-permute-start.1 = (bf16[256,768]{1,0:T(8,128)(2,1)S(1)}, bf16[256,768]{1,0:T(8,128)(2,1)S(1)}, u32[]{:S(2)}, u32[]{:S(2)}) collective-permute-start(bf16[256,768]{1,0:T(8,128)(2,1)S(1)} %collective-permute-done.refs_2_.refs_3_.refs_0_.refs_1_), channel_id=1, source_target_pairs={{0,1},{1,0},{2,3},{3,2},{4,5},{5,4},{6,7},{7,6},{8,9},{9,8},{10,11... | collective-permute-start | bytes 1179656 | tf_op jit(solution)/shard_map/ppermute | solution.py:56
  33.0 14.6 %collective-permute-start.9 = (bf16[208,768]{1,0:T(8,128)(2,1)S(1)}, bf16[208,768]{1,0:T(8,128)(2,1)S(1)}, u32[]{:S(2)}, u32[]{:S(2)}) collective-permute-start(bf16[208,768]{1,0:T(8,128)(2,1)S(1)} %collective-permute-done.6.refs_1_), channel_id=1, source_target_pairs={{0,1},{1,0},{2,3},{3,2},{4,5},{5,4},{6,7},{7,6},{8,9},{9,8},{10,11... | collective-permute-start | bytes 958472 | tf_op jit(solution)/shard_map/ppermute | solution.py:56
  47.7 18.6 %collective-permute-start.11 = (bf16[432,768]{1,0:T(8,128)(2,1)S(1)}, bf16[432,768]{1,0:T(8,128)(2,1)S(1)}, u32[]{:S(2)}, u32[]{:S(2)}) collective-permute-start(bf16[432,768]{1,0:T(8,128)(2,1)S(1)} %get-tuple-element.110.refs_9_), channel_id=1, source_target_pairs={{0,8},{1,9},{2,10},{3,11},{4,12},{5,13},{6,14},{7,15},{8,0},{9,1},... | collective-permute-start | bytes 1990664 | tf_op jit(solution)/shard_map/ppermute | solution.py:56
  48.0 18.3 %collective-permute-start.12 = (bf16[400,768]{1,0:T(8,128)(2,1)S(1)}, bf16[400,768]{1,0:T(8,128)(2,1)S(1)}, u32[]{:S(2)}, u32[]{:S(2)}) collective-permute-start(bf16[400,768]{1,0:T(8,128)(2,1)S(1)} %get-tuple-element.112), channel_id=1, source_target_pairs={{0,16},{1,17},{2,18},{3,19},{4,20},{5,21},{6,22},{7,23},{8,24},{9,... | collective-permute-start | bytes 1843208 | tf_op jit(solution)/shard_map/ppermute | solution.py:56
  48.2 6.7 %collective-permute-start.2 = (bf16[256,768]{1,0:T(8,128)(2,1)S(1)}, bf16[256,768]{1,0:T(8,128)(2,1)S(1)}, u32[]{:S(2)}, u32[]{:S(2)}) collective-permute-start(bf16[256,768]{1,0:T(8,128)(2,1)S(1)} %collective-permute-done.refs_2_.refs_3_.refs_0_.refs_1_), channel_id=1, source_target_pairs={{0,4},{1,5},{2,6},{3,7},{4,0},{5,1},{6,2},{7,3},{8,12},{9,13},{10,... | collective-permute-start | bytes 1179656 | tf_op jit(solution)/shard_map/ppermute | solution.py:56
  51.1 14.2 %collective-permute-start.14 = (bf16[256,768]{1,0:T(8,128)(2,1)S(1)}, bf16[256,768]{1,0:T(8,128)(2,1)S(1)}, u32[]{:S(2)}, u32[]{:S(2)}) collective-permute-start(bf16[256,768]{1,0:T(8,128)(2,1)S(1)} %bitcast.12), channel_id=1, source_target_pairs={{0,0},{1,1},{2,4},{3,5},{4,2},{5,3},{6,6},{7,7},{8,8},{9,9},{10,12... | collective-permute-start | bytes 1179656 | tf_op jit(solution)/shard_map/ppermute | solution.py:67
  66.5 9.4 %collective-permute-start.16 = (bf16[2288,768]{1,0:T(8,128)(2,1)S(1)}, bf16[2288,768]{1,0:T(8,128)(2,1)S(1)}, u32[]{:S(2)}, u32[]{:S(2)}) collective-permute-start(bf16[2288,768]{1,0:T(8,128)(2,1)S(1)} %held.1.refs_5_.refs_1_), channel_id=1, source_target_pairs={{0,4},{1,5},{2,6},{3,7},{4,0},{5,1},{6,2},{7,3},{8,12},{9,13},{10,... | collective-permute-start | bytes 10543112 | tf_op jit(solution)/shard_map/ppermute | solution.py:56
  66.7 6.1 %collective-permute-start.10 = (bf16[768,128]{1,0:T(8,128)(2,1)S(1)}, bf16[768,128]{1,0:T(8,128)(2,1)S(1)}, u32[]{:S(2)}, u32[]{:S(2)}) collective-permute-start(bf16[768,128]{1,0:T(8,128)(2,1)S(1)} %get-tuple-element.111), channel_id=1, source_target_pairs={{0,1},{1,0},{2,3},{3,2},{4,5},{5,4},{6,7},{7,6},{8,9},{9,8},{10,11... | collective-permute-start | bytes 589832 | tf_op jit(solution)/shard_map/ppermute | solution.py:56
  67.6 5.8 %collective-permute-start.18 = (bf16[112,768]{1,0:T(8,128)(2,1)S(1)}, bf16[112,768]{1,0:T(8,128)(2,1)S(1)}, u32[]{:S(2)}, u32[]{:S(2)}) collective-permute-start(bf16[112,768]{1,0:T(8,128)(2,1)S(1)} %get-tuple-element.120), channel_id=1, source_target_pairs={{0,8},{1,9},{2,10},{3,11},{4,12},{5,13},{6,14},{7,15},{8,0},{9,1},... | collective-permute-start | bytes 516104 | tf_op jit(solution)/shard_map/ppermute | solution.py:56
  85.0 6.7 %collective-permute-start.24 = (bf16[2,4,2,96,768]{4,3,2,1,0:T(8,128)(2,1)S(1)}, bf16[2,4,2,96,768]{4,3,2,1,0:T(8,128)(2,1)S(1)}, u32[]{:S(2)}, u32[]{:S(2)}) collective-permute-start(bf16[2,4,2,96,768]{4,3,2,1,0:T(8,128)(2,1)S(1)} %get-tuple-element.140), channel_id=1, source_target_pairs={{0,4},{1,5},{2,6},{3,7},{4,0},{5,1},{6,2},{7,3},{8,12},{9,13},{10,... | collective-permute-start | bytes 7077896 | tf_op jit(solution)/shard_map/ppermute | solution.py:56
  91.0 17.0 %collective-permute-start.25 = (bf16[2,4,2,96,768]{4,3,2,1,0:T(8,128)(2,1)S(1)}, bf16[2,4,2,96,768]{4,3,2,1,0:T(8,128)(2,1)S(1)}, u32[]{:S(2)}, u32[]{:S(2)}) collective-permute-start(bf16[2,4,2,96,768]{4,3,2,1,0:T(8,128)(2,1)S(1)} %get-tuple-element.147), channel_id=1, source_target_pairs={{0,4},{1,5},{2,6},{3,7},{4,0},{5,1},{6,2},{7,3},{8,12},{9,13},{10,... | collective-permute-start | bytes 7077896 | tf_op jit(solution)/shard_map/ppermute | solution.py:56
  91.2 10.5 %collective-permute-start.23 = (bf16[768,384]{1,0:T(8,128)(2,1)S(1)}, bf16[768,384]{1,0:T(8,128)(2,1)S(1)}, u32[]{:S(2)}, u32[]{:S(2)}) collective-permute-start(bf16[768,384]{1,0:T(8,128)(2,1)S(1)} %get-tuple-element.138), channel_id=1, source_target_pairs={{0,4},{1,5},{2,6},{3,7},{4,0},{5,1},{6,2},{7,3},{8,12},{9,13},{10,... | collective-permute-start | bytes 1769480 | tf_op jit(solution)/shard_map/ppermute | solution.py:56
  91.9 16.2 %collective-permute-start.27 = (bf16[2,2,96,768]{3,2,1,0:T(8,128)(2,1)S(1)}, bf16[2,2,96,768]{3,2,1,0:T(8,128)(2,1)S(1)}, u32[]{:S(2)}, u32[]{:S(2)}) collective-permute-start(bf16[2,2,96,768]{3,2,1,0:T(8,128)(2,1)S(1)} %get-tuple-element.148), channel_id=1, source_target_pairs={{0,16},{1,17},{2,18},{3,19},{4,20},{5,21},{6,22},{7,23},{8,24},{9,... | collective-permute-start | bytes 1769480 | tf_op jit(solution)/shard_map/ppermute | solution.py:56
  93.2 14.9 %collective-permute-start.26 = (bf16[2,2,96,768]{3,2,1,0:T(8,128)(2,1)S(1)}, bf16[2,2,96,768]{3,2,1,0:T(8,128)(2,1)S(1)}, u32[]{:S(2)}, u32[]{:S(2)}) collective-permute-start(bf16[2,2,96,768]{3,2,1,0:T(8,128)(2,1)S(1)} %get-tuple-element.141.refs_12_), channel_id=1, source_target_pairs={{0,8},{1,9},{2,10},{3,11},{4,12},{5,13},{6,14},{7,15},{8,0},{9,1},... | collective-permute-start | bytes 1769480 | tf_op jit(solution)/shard_map/ppermute | solution.py:56
  94.4 5.7 %collective-permute-start.20 = (bf16[768,128]{1,0:T(8,128)(2,1)S(1)}, bf16[768,128]{1,0:T(8,128)(2,1)S(1)}, u32[]{:S(2)}, u32[]{:S(2)}) collective-permute-start(bf16[768,128]{1,0:T(8,128)(2,1)S(1)} %get-tuple-element.135.refs_2_), channel_id=1, source_target_pairs={{0,1},{1,0},{2,3},{3,2},{4,5},{5,4},{6,7},{7,6},{8,9},{9,8},{10,11... | collective-permute-start | bytes 589832 | tf_op jit(solution)/shard_map/ppermute | solution.py:56
  102.7 16.2 %collective-permute-start.28 = (bf16[768,192]{1,0:T(8,128)(2,1)S(1)}, bf16[768,192]{1,0:T(8,128)(2,1)S(1)}, u32[]{:S(2)}, u32[]{:S(2)}) collective-permute-start(bf16[768,192]{1,0:T(8,128)(2,1)S(1)} %get-tuple-element.155), channel_id=1, source_target_pairs={{0,1},{1,0},{2,3},{3,2},{4,5},{5,4},{6,7},{7,6},{8,9},{9,8},{10,11... | collective-permute-start | bytes 884744 | tf_op jit(solution)/shard_map/ppermute | solution.py:56
  108.6 20.4 %collective-permute-start.32 = (bf16[6,96,768]{2,1,0:T(8,128)(2,1)S(1)}, bf16[6,96,768]{2,1,0:T(8,128)(2,1)S(1)}, u32[]{:S(2)}, u32[]{:S(2)}) collective-permute-start(bf16[6,96,768]{2,1,0:T(8,128)(2,1)S(1)} %get-tuple-element.164), channel_id=1, source_target_pairs={{0,16},{1,17},{2,18},{3,19},{4,20},{5,21},{6,22},{7,23},{8,24},{9,... | collective-permute-start | bytes 2654216 | tf_op jit(solution)/shard_map/ppermute | solution.py:56
  108.9 20.1 %collective-permute-start.31 = (bf16[6,96,768]{2,1,0:T(8,128)(2,1)S(1)}, bf16[6,96,768]{2,1,0:T(8,128)(2,1)S(1)}, u32[]{:S(2)}, u32[]{:S(2)}) collective-permute-start(bf16[6,96,768]{2,1,0:T(8,128)(2,1)S(1)} %get-tuple-element.149.refs_11_), channel_id=1, source_target_pairs={{0,8},{1,9},{2,10},{3,11},{4,12},{5,13},{6,14},{7,15},{8,0},{9,1},... | collective-permute-start | bytes 2654216 | tf_op jit(solution)/shard_map/ppermute | solution.py:56
  122.5 8.3 %collective-permute-start.34 = (bf16[512,768]{1,0:T(8,128)(2,1)S(1)}, bf16[512,768]{1,0:T(8,128)(2,1)S(1)}, u32[]{:S(2)}, u32[]{:S(2)}) collective-permute-start(bf16[512,768]{1,0:T(8,128)(2,1)S(1)} %get-tuple-element.168), channel_id=1, source_target_pairs={{0,4},{1,5},{2,6},{3,7},{4,0},{5,1},{6,2},{7,3},{8,12},{9,13},{10,... | collective-permute-start | bytes 2359304 | tf_op jit(solution)/shard_map/ppermute | solution.py:56
  124.3 11.4 %collective-permute-start.29 = (bf16[416,384]{1,0:T(8,128)(2,1)S(1)}, bf16[416,384]{1,0:T(8,128)(2,1)S(1)}, u32[]{:S(2)}, u32[]{:S(2)}) collective-permute-start(bf16[416,384]{1,0:T(8,128)(2,1)S(1)} %get-tuple-element.161), channel_id=1, source_target_pairs={{0,8},{1,9},{2,10},{3,11},{4,12},{5,13},{6,14},{7,15},{8,0},{9,1},... | collective-permute-start | bytes 958472 | tf_op jit(solution)/shard_map/ppermute | solution.py:56
  124.6 11.3 %collective-permute-start.30 = (bf16[416,384]{1,0:T(8,128)(2,1)S(1)}, bf16[416,384]{1,0:T(8,128)(2,1)S(1)}, u32[]{:S(2)}, u32[]{:S(2)}) collective-permute-start(bf16[416,384]{1,0:T(8,128)(2,1)S(1)} %get-tuple-element.163), channel_id=1, source_target_pairs={{0,16},{1,17},{2,18},{3,19},{4,20},{5,21},{6,22},{7,23},{8,24},{9,... | collective-permute-start | bytes 958472 | tf_op jit(solution)/shard_map/ppermute | solution.py:56
  129.3 5.9 %collective-permute-start.33 = (bf16[2,96,768]{2,1,0:T(8,128)(2,1)S(1)}, bf16[2,96,768]{2,1,0:T(8,128)(2,1)S(1)}, u32[]{:S(2)}, u32[]{:S(2)}) collective-permute-start(bf16[2,96,768]{2,1,0:T(8,128)(2,1)S(1)} %get-tuple-element.167), channel_id=1, source_target_pairs={{0,1},{1,0},{2,3},{3,2},{4,5},{5,4},{6,7},{7,6},{8,9},{9,8},{10,11... | collective-permute-start | bytes 884744 | tf_op jit(solution)/shard_map/ppermute | solution.py:56
  130.4 11.6 %collective-permute-start.38 = (bf16[2,96,768]{2,1,0:T(8,128)(2,1)S(1)}, bf16[2,96,768]{2,1,0:T(8,128)(2,1)S(1)}, u32[]{:S(2)}, u32[]{:S(2)}) collective-permute-start(bf16[2,96,768]{2,1,0:T(8,128)(2,1)S(1)} %get-tuple-element.172), channel_id=1, source_target_pairs={{0,8},{1,9},{2,10},{3,11},{4,12},{5,13},{6,14},{7,15},{8,0},{9,1},... | collective-permute-start | bytes 884744 | tf_op jit(solution)/shard_map/ppermute | solution.py:56
  130.8 12.0 %collective-permute-start.37 = (bf16[2,96,768]{2,1,0:T(8,128)(2,1)S(1)}, bf16[2,96,768]{2,1,0:T(8,128)(2,1)S(1)}, u32[]{:S(2)}, u32[]{:S(2)}) collective-permute-start(bf16[2,96,768]{2,1,0:T(8,128)(2,1)S(1)} %get-tuple-element.169.refs_2_), channel_id=1, source_target_pairs={{0,16},{1,17},{2,18},{3,19},{4,20},{5,21},{6,22},{7,23},{8,24},{9,... | collective-permute-start | bytes 884744 | tf_op jit(solution)/shard_map/ppermute | solution.py:56
  135.9 9.5 %collective-permute-start.35 = (bf16[224,384]{1,0:T(8,128)(2,1)S(1)}, bf16[224,384]{1,0:T(8,128)(2,1)S(1)}, u32[]{:S(2)}, u32[]{:S(2)}) collective-permute-start(bf16[224,384]{1,0:T(8,128)(2,1)S(1)} %get-tuple-element.170.refs_6_), channel_id=1, source_target_pairs={{0,16},{1,17},{2,18},{3,19},{4,20},{5,21},{6,22},{7,23},{8,24},{9,... | collective-permute-start | bytes 516104 | tf_op jit(solution)/shard_map/ppermute | solution.py:56
  137.1 6.5 %collective-permute-start.39 = (bf16[96,768]{1,0:T(8,128)(2,1)S(1)}, bf16[96,768]{1,0:T(8,128)(2,1)S(1)}, u32[]{:S(2)}, u32[]{:S(2)}) collective-permute-start(bf16[96,768]{1,0:T(8,128)(2,1)S(1)} %far_back.1.refs_4_), channel_id=1, source_target_pairs={{0,2},{1,3},{2,0},{3,1},{4,6},{5,7},{6,4},{7,5},{8,10},{9,11},{10,... | collective-permute-start | bytes 442376 | tf_op jit(solution)/shard_map/ppermute | solution.py:56
  138.7 6.4 %collective-permute-start.36 = (bf16[192,384]{1,0:T(8,128)(2,1)S(1)}, bf16[192,384]{1,0:T(8,128)(2,1)S(1)}, u32[]{:S(2)}, u32[]{:S(2)}) collective-permute-start(bf16[192,384]{1,0:T(8,128)(2,1)S(1)} %get-tuple-element.171), channel_id=1, source_target_pairs={{0,8},{1,9},{2,10},{3,11},{4,12},{5,13},{6,14},{7,15},{8,0},{9,1},... | collective-permute-start | bytes 442376 | tf_op jit(solution)/shard_map/ppermute | solution.py:56
  142.0 23.3 %collective-permute-start.42 = (bf16[256,768]{1,0:T(8,128)(2,1)S(1)}, bf16[256,768]{1,0:T(8,128)(2,1)S(1)}, u32[]{:S(2)}, u32[]{:S(2)}) collective-permute-start(bf16[256,768]{1,0:T(8,128)(2,1)S(1)} %near.1.refs_2_), channel_id=1, source_target_pairs={{0,1},{1,0},{2,3},{3,2},{4,5},{5,4},{6,7},{7,6},{8,9},{9,8},{10,11... | collective-permute-start | bytes 1179656 | tf_op jit(solution)/shard_map/ppermute | solution.py:56
  145.6 19.8 %collective-permute-start.40 = (bf16[208,768]{1,0:T(8,128)(2,1)S(1)}, bf16[208,768]{1,0:T(8,128)(2,1)S(1)}, u32[]{:S(2)}, u32[]{:S(2)}) collective-permute-start(bf16[208,768]{1,0:T(8,128)(2,1)S(1)} %qkv_three.1.refs_2_.refs_0_), channel_id=1, source_target_pairs={{0,2},{1,3},{2,0},{3,1},{4,6},{5,7},{6,4},{7,5},{8,10},{9,11},{10,... | collective-permute-start | bytes 958472 | tf_op jit(solution)/shard_map/ppermute | solution.py:56
  147.2 18.1 %collective-permute-start.41 = (bf16[2,96,768]{2,1,0:T(8,128)(2,1)S(1)}, bf16[2,96,768]{2,1,0:T(8,128)(2,1)S(1)}, u32[]{:S(2)}, u32[]{:S(2)}) collective-permute-start(bf16[2,96,768]{2,1,0:T(8,128)(2,1)S(1)} %get-tuple-element.174), channel_id=1, source_target_pairs={{0,1},{1,0},{2,3},{3,2},{4,5},{5,4},{6,7},{7,6},{8,9},{9,8},{10,11... | collective-permute-start | bytes 884744 | tf_op jit(solution)/shard_map/ppermute | solution.py:56
  165.5 8.1 %collective-permute-start.43 = (bf16[208,768]{1,0:T(8,128)(2,1)S(1)}, bf16[208,768]{1,0:T(8,128)(2,1)S(1)}, u32[]{:S(2)}, u32[]{:S(2)}) collective-permute-start(bf16[208,768]{1,0:T(8,128)(2,1)S(1)} %qkv_four.1.refs_0_), channel_id=1, source_target_pairs={{0,1},{1,0},{2,3},{3,2},{4,5},{5,4},{6,7},{7,6},{8,9},{9,8},{10,11... | collective-permute-start | bytes 958472 | tf_op jit(solution)/shard_map/ppermute | solution.py:56
  165.6 6.0 %collective-permute-start.45 = (bf16[192,768]{1,0:T(8,128)(2,1)S(1)}, bf16[192,768]{1,0:T(8,128)(2,1)S(1)}, u32[]{:S(2)}, u32[]{:S(2)}) collective-permute-start(bf16[192,768]{1,0:T(8,128)(2,1)S(1)} %slice.14), channel_id=1, source_target_pairs={{0,16},{1,17},{2,18},{3,19},{4,20},{5,21},{6,22},{7,23},{8,24},{9,... | collective-permute-start | bytes 884744 | tf_op jit(solution)/shard_map/ppermute | solution.py:56
  167.4 5.9 %collective-permute-start.44 = (bf16[192,768]{1,0:T(8,128)(2,1)S(1)}, bf16[192,768]{1,0:T(8,128)(2,1)S(1)}, u32[]{:S(2)}, u32[]{:S(2)}) collective-permute-start(bf16[192,768]{1,0:T(8,128)(2,1)S(1)} %slice.14), channel_id=1, source_target_pairs={{0,8},{1,9},{2,10},{3,11},{4,12},{5,13},{6,14},{7,15},{8,0},{9,1},... | collective-permute-start | bytes 884744 | tf_op jit(solution)/shard_map/ppermute | solution.py:56
  167.6 8.0 %collective-permute-start.48 = (bf16[96,768]{1,0:T(8,128)(2,1)S(1)}, bf16[96,768]{1,0:T(8,128)(2,1)S(1)}, u32[]{:S(2)}, u32[]{:S(2)}) collective-permute-start(bf16[96,768]{1,0:T(8,128)(2,1)S(1)} %far_in.1.refs_2_), channel_id=1, source_target_pairs={{0,2},{1,3},{2,0},{3,1},{4,6},{5,7},{6,4},{7,5},{8,10},{9,11},{10,... | collective-permute-start | bytes 442376 | tf_op jit(solution)/shard_map/ppermute | solution.py:56
  173.6 22.6 %collective-permute-start.47 = (bf16[288,768]{1,0:T(8,128)(2,1)S(1)}, bf16[288,768]{1,0:T(8,128)(2,1)S(1)}, u32[]{:S(2)}, u32[]{:S(2)}) collective-permute-start(bf16[288,768]{1,0:T(8,128)(2,1)S(1)} %get-tuple-element.176), channel_id=1, source_target_pairs={{0,16},{1,17},{2,18},{3,19},{4,20},{5,21},{6,22},{7,23},{8,24},{9,... | collective-permute-start | bytes 1327112 | tf_op jit(solution)/shard_map/ppermute | solution.py:56
  174.7 21.5 %collective-permute-start.46 = (bf16[288,768]{1,0:T(8,128)(2,1)S(1)}, bf16[288,768]{1,0:T(8,128)(2,1)S(1)}, u32[]{:S(2)}, u32[]{:S(2)}) collective-permute-start(bf16[288,768]{1,0:T(8,128)(2,1)S(1)} %get-tuple-element.175.refs_6_), channel_id=1, source_target_pairs={{0,8},{1,9},{2,10},{3,11},{4,12},{5,13},{6,14},{7,15},{8,0},{9,1},... | collective-permute-start | bytes 1327112 | tf_op jit(solution)/shard_map/ppermute | solution.py:56
  175.7 11.1 %collective-permute-start.50 = (bf16[2,96,768]{2,1,0:T(8,128)(2,1)S(1)}, bf16[2,96,768]{2,1,0:T(8,128)(2,1)S(1)}, u32[]{:S(2)}, u32[]{:S(2)}) collective-permute-start(bf16[2,96,768]{2,1,0:T(8,128)(2,1)S(1)} %last.1.refs_5_.refs_6_), channel_id=1, source_target_pairs={{0,16},{1,17},{2,18},{3,19},{4,20},{5,21},{6,22},{7,23},{8,24},{9,... | collective-permute-start | bytes 884744 | tf_op jit(solution)/shard_map/ppermute | solution.py:56
  175.9 20.4 %collective-permute-start.49 = (bf16[2,96,768]{2,1,0:T(8,128)(2,1)S(1)}, bf16[2,96,768]{2,1,0:T(8,128)(2,1)S(1)}, u32[]{:S(2)}, u32[]{:S(2)}) collective-permute-start(bf16[2,96,768]{2,1,0:T(8,128)(2,1)S(1)} %last.1.refs_5_.refs_6_), channel_id=1, source_target_pairs={{0,8},{1,9},{2,10},{3,11},{4,12},{5,13},{6,14},{7,15},{8,0},{9,1},... | collective-permute-start | bytes 884744 | tf_op jit(solution)/shard_map/ppermute | solution.py:56
  177.0 21.0 %collective-permute-start.53 = (bf16[256,768]{1,0:T(8,128)(2,1)S(1)}, bf16[256,768]{1,0:T(8,128)(2,1)S(1)}, u32[]{:S(2)}, u32[]{:S(2)}) collective-permute-start(bf16[256,768]{1,0:T(8,128)(2,1)S(1)} %get-tuple-element.181), channel_id=1, source_target_pairs={{0,0},{1,1},{2,4},{3,5},{4,2},{5,3},{6,6},{7,7},{8,8},{9,9},{10,12... | collective-permute-start | bytes 1179656 | tf_op jit(solution)/shard_map/ppermute | solution.py:67
  186.9 19.0 %collective-permute-start.54 = (bf16[256,768]{1,0:T(8,128)(2,1)S(1)}, bf16[256,768]{1,0:T(8,128)(2,1)S(1)}, u32[]{:S(2)}, u32[]{:S(2)}) collective-permute-start(bf16[256,768]{1,0:T(8,128)(2,1)S(1)} %get-tuple-element.182), channel_id=1, source_target_pairs={{0,0},{1,1},{2,4},{3,5},{4,2},{5,3},{6,6},{7,7},{8,8},{9,9},{10,12... | collective-permute-start | bytes 1179656 | tf_op jit(solution)/shard_map/ppermute | solution.py:67
  196.3 9.6 %collective-permute-start.51 = (bf16[192,768]{1,0:T(8,128)(2,1)S(1)}, bf16[192,768]{1,0:T(8,128)(2,1)S(1)}, u32[]{:S(2)}, u32[]{:S(2)}) collective-permute-start(bf16[192,768]{1,0:T(8,128)(2,1)S(1)} %get-tuple-element.177), channel_id=1, source_target_pairs={{0,8},{1,9},{2,10},{3,11},{4,12},{5,13},{6,14},{7,15},{8,0},{9,1},... | collective-permute-start | bytes 884744 | tf_op jit(solution)/shard_map/ppermute | solution.py:56
  196.7 9.2 %collective-permute-start.52 = (bf16[192,768]{1,0:T(8,128)(2,1)S(1)}, bf16[192,768]{1,0:T(8,128)(2,1)S(1)}, u32[]{:S(2)}, u32[]{:S(2)}) collective-permute-start(bf16[192,768]{1,0:T(8,128)(2,1)S(1)} %get-tuple-element.178), channel_id=1, source_target_pairs={{0,16},{1,17},{2,18},{3,19},{4,20},{5,21},{6,22},{7,23},{8,24},{9,... | collective-permute-start | bytes 884744 | tf_op jit(solution)/shard_map/ppermute | solution.py:56
  206.1 6.3 %collective-permute-start.55 = (bf16[2320,768]{1,0:T(8,128)(2,1)S(1)}, bf16[2320,768]{1,0:T(8,128)(2,1)S(1)}, u32[]{:S(2)}, u32[]{:S(2)}) collective-permute-start(bf16[2320,768]{1,0:T(8,128)(2,1)S(1)} %plane.1), channel_id=1, source_target_pairs={{0,4},{1,5},{2,6},{3,7},{4,0},{5,1},{6,2},{7,3},{8,12},{9,13},{10,... | collective-permute-start | bytes 10690568 | tf_op jit(solution)/shard_map/ppermute | solution.py:56
  (26 other events, 123.5 us)
where the time goes:
time: 220 us; the launch traced here: 218 us
  waiting for transfers between devices  81.6 us (37%)
  starting transfers between devices  72.1 us (33%)
  Pallas kernels  56.5 us (26%)
  local copies, waits for them, and re-layouts  5.77 us (3%)
    ppermute x52, waiting for transfers between devices, hop(): return lax.ppermute(array, ('dp', 'tp'), pairs)  73.4 us
    pallas_call x35, Pallas kernels, call(): return lambda *arrays: run(*arrays, *deps)  48.1 us
    ppermute x52, starting transfers between devices, hop(): return lax.ppermute(array, ('dp', 'tp'), pairs)  43.3 us
    ppermute x4, starting transfers between devices, place(): return lax.ppermute(array, ('dp', 'tp'), pairs)  28.7 us
    ppermute x4, waiting for transfers between devices, place(): return lax.ppermute(array, ('dp', 'tp'), pairs)  8.25 us
    unnamed x37, local copies, waits for them, and re-layouts  5.45 us
    pallas_call x1, Pallas kernels, per_device(): pl.pallas_call(second_half_kernel, out_shape=as_shape(halves_out + [squar...  4.86 us
  transfers between devices with their start and end apart: 56, of which 22 were waited for; matrix products, arithmetic and copies ran while one was open for 0% of the time, Pallas kernels for 20%

commit v1 on v0

--- a/solution.py
+++ b/solution.py
@@ -180,11 +180,11 @@
 
 
 def attention_back_kernel(
-    h, info, rnd_own, rnd_other, q_ref, k_ref, v_ref, lse_ref, g0, g1, g2, g3, out_ref, sums_ref, do_scr, dk_scr, dv_scr, dq_scr
+    h, info, rnd_own, rnd_other, q_ref, k_ref, v_ref, lse_ref, g0, g13, g2, out_ref, sums_ref, do_scr, dk_scr, dv_scr, dq_scr
 ):
     quarter, native = info[0], info[4]
-    for slot, g_ref in enumerate((g0, g1, g2, g3)):
-        do_scr[slot * QUARTER : (slot + 1) * QUARTER, :] = unpack_heads(g_ref, 0)[h]
+    for slot, (g_ref, row) in enumerate(((g0, 0), (g13, 0), (g2, 0), (g13, PACKED))):
+        do_scr[slot * QUARTER : (slot + 1) * QUARTER, :] = unpack_heads(g_ref, row)[h]
     keys = k_ref[...]
     keys_t = keys.T
     values = v_ref[...]
@@ -343,7 +343,7 @@
 
 def ffn_back_kernel(info, first_ref, second_ref, gb_ref, gp_ref, gain_one_ref, vec_in, *rest):
     w_out_s, w_in_ref, w_back_ref, w_in_s, w_back_s, x_ref, att_ref = rest[:7]
-    g0, g13, g2, gin_ref, vec_ref, keep, send, go_keep, go_send = rest[7:16]
+    g0, g1, g23, gin_ref, vec_ref, keep, send, go_keep, go_send = rest[7:16]
     gpre_ref, flip_scr, lhs_scr = rest[16:]
     grad_branch = gb_ref[...]
     grad_first = second_ref[...]
@@ -363,7 +363,7 @@
     grad_mixed = grad_in.astype(bf16)
     vec_ref[5:6, :] = jnp.sum(grad_mixed.astype(f32), axis=0, keepdims=True)
     grad_att = mm_nt(grad_mixed, w_out_s[...]).astype(bf16)
-    for slot, (g_ref, row_at) in enumerate(((g0, 0), (g13, 0), (g2, 0), (g13, PACKED))):
+    for slot, (g_ref, row_at) in enumerate(((g0, 0), (g1, 0), (g23, 0), (g23, PACKED))):
         lo = slot * GROUP_WIDTH
         pack_heads(
             g_ref, row_at, [grad_att[:, lo + h * HEAD_DIM : lo + (h + 1) * HEAD_DIM] for h in range(GROUP)]
@@ -547,6 +547,11 @@
 def last_mix_kernel(by_x, by_y, to_x, to_y):
     to_x[...] = by_y[CUT:PIECE]
     to_y[...] = by_x[:CUT]
+
+
+def to_z_kernel(own, other, out):
+    out[:PACKED] = own[...]
+    out[PACKED:] = other[PACKED:]
 
 
 def level_one_kernel(keep, other, first, second):
@@ -865,10 +870,10 @@
     )(info, grad_branch, activated)
     back_other = hop(back_send, CORE, 0)
 
-    g0, g13, g2, grad_in, vectors, in_keep, in_send, go_keep, go_send = call(
+    g0, g1_send, g23, grad_in, vectors, in_keep, in_send, go_keep, go_send = call(
         ffn_back_kernel,
         [SMEM] + [VMEM] * 13,
-        [packed, double, packed, rows_f32, vec_rows] + [pairs] * 2 + [halves] * 2,
+        [packed, packed, double, rows_f32, vec_rows] + [pairs] * 2 + [halves] * 2,
         [pltpu.VMEM((QUARTER, TP * WIDTH), bf16)] + flips,
         20,
         "ffn_back",
@@ -889,15 +894,14 @@
         ffn_input,
         attended,
     )
-    g1 = hop(g13, 0, 1)
-    g2 = hop(g2, CORE, 0)
-    g3 = hop(g1[PACKED:], CORE, 0)
+    g2 = hop(g23, CORE, 0)
+    g13 = hop(step(to_z_kernel, "to_z", [double[0]], g1_send, g2), 0, 1)
 
     first_level = [(2, 2, SLICE, WIDTH)] * 2
     def hop_pair(pair, first, second):
         return hop(pair[0], first, 0), hop(pair[1], second, 0)
 
-    back_sums = step(level_one_kernel, "back_one", first_level, back_keep, back_other, deps=(g13,))
+    back_sums = step(level_one_kernel, "back_one", first_level, back_keep, back_other, deps=(g0,))
     back_x, back_y = hop_pair(back_sums, X_BIT, Y_BIT)
     in_other = hop(in_send, CORE, 0)
     go_other = hop(go_send, CORE, 0)
@@ -905,7 +909,7 @@
     def head_back(h, deps):
         return call(
             functools.partial(attention_back_kernel, h),
-            [SMEM] * 3 + [VMEM] * 8,
+            [SMEM] * 3 + [VMEM] * 7,
             [((LENGTH, 3 * HEAD_DIM), bf16), ((8, 3 * HEAD_DIM), f32)],
             [
                 pltpu.VMEM((LENGTH, HEAD_DIM), bf16),
@@ -916,7 +920,7 @@
             12,
             f"attention_back_{h}",
             deps,
-        )(info, random_own, random_other, *heads[3 * h : 3 * h + 3], lse, g0, g1, g2, g3)
+        )(info, random_own, random_other, *heads[3 * h : 3 * h + 3], lse, g0, g13, g2)
 
     go_own, go_send = step(go_kernel, "go", [(WIDTH, GROUP_WIDTH)] * 2, go_keep, go_other)
     go_near = hop(go_send, 0, 1)

time: 220 us -> 221 us (level)
    ppermute x52 -> x51, starting transfers between devices: 43.3 us -> 44.5 us  [hop(): return lax.ppermute(array, ('dp', 'tp'), pairs)]
    ppermute x52 -> x51, waiting for transfers between devices: 73.4 us -> 72.7 us  [hop(): return lax.ppermute(array, ('dp', 'tp'), pairs)]
    pallas_call x35 -> x36, Pallas kernels: 48.1 us -> 47.9 us  [call(): return lambda *arrays: run(*arrays, *deps)]
  transfers between devices with their start and end apart: 56 -> 55, of which waited for: 22 -> 20; matrix products, arithmetic and copies ran while one was open for 0% -> 0% of each run, Pallas kernels for 20% -> 20%
where the time goes in v1:
time: 221 us; the launch traced here: 218 us
  waiting for transfers between devices  80.6 us (36%)
  starting transfers between devices  74.2 us (34%)
  Pallas kernels  56.3 us (25%)
  local copies, waits for them, and re-layouts  5.76 us (3%)
    ppermute x51, waiting for transfers between devices, hop(): return lax.ppermute(array, ('dp', 'tp'), pairs)  72.7 us
    pallas_call x36, Pallas kernels, call(): return lambda *arrays: run(*arrays, *deps)  47.9 us
    ppermute x51, starting transfers between devices, hop(): return lax.ppermute(array, ('dp', 'tp'), pairs)  44.5 us
    ppermute x4, starting transfers between devices, place(): return lax.ppermute(array, ('dp', 'tp'), pairs)  29.6 us
    ppermute x4, waiting for transfers between devices, place(): return lax.ppermute(array, ('dp', 'tp'), pairs)  7.9 us
    unnamed x37, local copies, waits for them, and re-layouts  5.45 us
    pallas_call x1, Pallas kernels, per_device(): pl.pallas_call(second_half_kernel, out_shape=as_shape(halves_out + [squar...  4.86 us
  transfers between devices with their start and end apart: 55, of which 20 were waited for; matrix products, arithmetic and copies ran while one was open for 0% of the time, Pallas kernels for 20%

profile of v1, /device:TPU:1, one launch (start us, length us, event | category | flops | bytes accessed | tf_op | source)
XLA Modules:
  0.0 218.4 jit_solution(4179811270248319868)
XLA Ops:
  0.7 5.7 %collective-permute-start = (bf16[256,768]{1,0:T(8,128)(2,1)}, bf16[256,768]{1,0:T(8,128)(2,1)S(1)}, u32[]{:S(2)}, u32[]{:S(2)}) collective-permute-start(bf16[256,768]{1,0:T(8,128)(2,1)} %bitcast.11), channel_id=1, source_target_pairs={{0,0},{1,1},{2,4},{3,5},{4,2},{5,3},{6,6},{7,7},{8,8},{9,9},{10,12... | collective-permute-start | bytes 1179656 | tf_op jit(solution)/shard_map/ppermute | solution.py:67
  6.5 1.3 copy-done
  7.8 1.3 copy-done.2
  11.0 1.4 collective-permute-start.5
  13.3 2.0 copy-done.4
  16.2 11.1 %collective-permute-done.6.refs_1_ = bf16[208,768]{1,0:T(8,128)(2,1)S(1)} collective-permute-done((bf16[208,768]{1,0:T(8,128)(2,1)S(1)}, bf16[208,768]{1,0:T(8,128)(2,1)S(1)}, u32[]{:S(2)}, u32[]{:S(2)}) %collective-permute-start.6) | collective-permute-done | bytes 319520 | tf_op jit(solution)/shard_map/ppermute | solution.py:56
  27.4 1.3 collective-permute-start.8
  29.9 3.1 %collective-permute-start.1 = (bf16[256,768]{1,0:T(8,128)(2,1)S(1)}, bf16[256,768]{1,0:T(8,128)(2,1)S(1)}, u32[]{:S(2)}, u32[]{:S(2)}) collective-permute-start(bf16[256,768]{1,0:T(8,128)(2,1)S(1)} %collective-permute-done.refs_2_.refs_3_.refs_0_.refs_1_), channel_id=1, source_target_pairs={{0,1},{1,0},{2,3},{3,2},{4,5},{5,4},{6,7},{7,6},{8,9},{9,8},{10,11... | collective-permute-start | bytes 1179656 | tf_op jit(solution)/shard_map/ppermute | solution.py:56
  33.0 14.5 %collective-permute-done.9.refs_2_.refs_3_ = bf16[208,768]{1,0:T(8,128)(2,1)S(1)} collective-permute-done((bf16[208,768]{1,0:T(8,128)(2,1)S(1)}, bf16[208,768]{1,0:T(8,128)(2,1)S(1)}, u32[]{:S(2)}, u32[]{:S(2)}) %collective-permute-start.9) | collective-permute-done | bytes 319520 | tf_op jit(solution)/shard_map/ppermute | solution.py:56
  48.2 2.9 %collective-permute-start.2 = (bf16[256,768]{1,0:T(8,128)(2,1)S(1)}, bf16[256,768]{1,0:T(8,128)(2,1)S(1)}, u32[]{:S(2)}, u32[]{:S(2)}) collective-permute-start(bf16[256,768]{1,0:T(8,128)(2,1)S(1)} %collective-permute-done.refs_2_.refs_3_.refs_0_.refs_1_), channel_id=1, source_target_pairs={{0,4},{1,5},{2,6},{3,7},{4,0},{5,1},{6,2},{7,3},{8,12},{9,13},{10,... | collective-permute-start | bytes 1179656 | tf_op jit(solution)/shard_map/ppermute | solution.py:56
  51.1 3.8 %collective-permute-start.14 = (bf16[256,768]{1,0:T(8,128)(2,1)S(1)}, bf16[256,768]{1,0:T(8,128)(2,1)S(1)}, u32[]{:S(2)}, u32[]{:S(2)}) collective-permute-start(bf16[256,768]{1,0:T(8,128)(2,1)S(1)} %bitcast.12), channel_id=1, source_target_pairs={{0,0},{1,1},{2,4},{3,5},{4,2},{5,3},{6,6},{7,7},{8,8},{9,9},{10,12... | collective-permute-start | bytes 1179656 | tf_op jit(solution)/shard_map/ppermute | solution.py:67
  54.9 9.9 %attention.1 = (bf16[384,128]{1,0:T(8,128)(2,1)S(1)}, bf16[768,128]{1,0:T(8,128)(2,1)S(1)}, bf16[384,128]{1,0:T(8,128)(2,1)S(1)}, bf16[1024,64]{1,0:T(8,128)(2,1...) custom-call(s32[5]{0:T(128)S(1)} %stack.27.refs_0_.info, ...), custom_call_target="tpu_custom_call" | custom-call | flops 1 | bytes 1 | tf_op jit(solution)/shard_map/attention/pallas_call | solution.py:697
  69.3 3.6 %collective-permute-done.10.refs_4_.refs_3_ = bf16[768,128]{1,0:T(8,128)(2,1)S(1)} collective-permute-done((bf16[768,128]{1,0:T(8,128)(2,1)S(1)}, bf16[768,128]{1,0:T(8,128)(2,1)S(1)}, u32[]{:S(2)}, u32[]{:S(2)}) %collective-permute-start.10) | collective-permute-done | bytes 196640 | tf_op jit(solution)/shard_map/ppermute | solution.py:56
  73.4 1.2 collective-permute-start.19
  77.1 5.8 %ffn.1 = (bf16[256,768]{1,0:T(8,128)(2,1)S(1)}, f32[256,768]{1,0:T(8,128)S(1)}, f32[256,768]{1,0:T(8,128)S(1)}, bf16[256,768]{1,0:T(8,128)(2,1)S(1)}, bf16[256,7...) custom-call(s32[5]{0:T(128)S(1)} %stack.27.refs_0_.info, ...), custom_call_target="tpu_custom_call" | custom-call | flops 1 | bytes 1 | tf_op jit(solution)/shard_map/ffn/pallas_call | solution.py:697
  82.9 2.1 back_grads.1
  85.4 5.6 %ffn_back.1 = (bf16[384,128]{1,0:T(8,128)(2,1)S(1)}, bf16[384,128]{1,0:T(8,128)(2,1)S(1)}, bf16[768,128]{1,0:T(8,128)(2,1)S(1)}, f32[256,768]{1,0:T(8,128)S(1)},...) custom-call(s32[5]{0:T(128)S(1)} %stack.27.refs_0_.info, ...), custom_call_target="tpu_custom_call" | custom-call | flops 1 | bytes 1 | tf_op jit(solution)/shard_map/ffn_back/pallas_call | solution.py:697
  91.9 1.3 collective-permute-start.26
  95.1 1.6 collective-permute-done.20.refs_1_.refs_9_
  96.8 1.3 collective-permute-start.21
  98.7 4.5 %collective-permute-done.21.refs_8_ = bf16[768,128]{1,0:T(8,128)(2,1)S(1)} collective-permute-done((bf16[768,128]{1,0:T(8,128)(2,1)S(1)}, bf16[768,128]{1,0:T(8,128)(2,1)S(1)}, u32[]{:S(2)}, u32[]{:S(2)}) %collective-permute-start.21) | collective-permute-done | bytes 196640 | tf_op jit(solution)/shard_map/ppermute | solution.py:56
  103.2 4.8 %attention_back_0.1 = (bf16[1024,192]{1,0:T(8,128)(2,1)S(1)}, f32[8,192]{1,0:T(8,128)S(1)}) custom-call(s32[5]{0:T(128)S(1)} %stack.27.refs_0_.info, s32[576]{0:T(1024)S(1)} %reshape.33.refs_1_, s32[576]{0:T(1024)S(1)} %collective-permute-done.4.refs_4_.refs_2_, bf16[1024,64]{1,0:T(8,128)(2,1)S(1)} %get-tuple-element.114.refs_3_, ...), custom_call_target="tpu_custom_call" | custom-call | flops 1 | bytes 1 | tf_op jit(solution)/shard_map/attention_back_0/pallas_call | solution.py:697
  108.6 1.3 collective-permute-start.31
  109.9 1.2 collective-permute-start.30
  111.1 4.5 %attention_back_1.1 = (bf16[1024,192]{1,0:T(8,128)(2,1)S(1)}, f32[8,192]{1,0:T(8,128)S(1)}) custom-call(s32[5]{0:T(128)S(1)} %stack.27.refs_0_.info, s32[576]{0:T(1024)S(1)} %reshape.33.refs_1_, s32[576]{0:T(1024)S(1)} %collective-permute-done.4.refs_4_.refs_2_, bf16[1024,64]{1,0:T(8,128)(2,1)S(1)} %get-tuple-element.143.refs_3_, ...), custom_call_target="tpu_custom_call" | custom-call | flops 1 | bytes 1 | tf_op jit(solution)/shard_map/attention_back_1/pallas_call | solution.py:697
  115.7 4.5 %attention_back_2.1 = (bf16[1024,192]{1,0:T(8,128)(2,1)S(1)}, f32[8,192]{1,0:T(8,128)S(1)}) custom-call(s32[5]{0:T(128)S(1)} %stack.27.refs_0_.info, s32[576]{0:T(1024)S(1)} %reshape.33.refs_1_, s32[576]{0:T(1024)S(1)} %collective-permute-done.4.refs_4_.refs_2_, bf16[1024,64]{1,0:T(8,128)(2,1)S(1)} %get-tuple-element.151.refs_3_, ...), custom_call_target="tpu_custom_call" | custom-call | flops 1 | bytes 1 | tf_op jit(solution)/shard_map/attention_back_2/pallas_call | solution.py:697
  120.2 2.1 qkv_grads.1
  122.3 1.5 token_grad.1
  123.8 2.1 collective-permute-start.33
  126.5 1.8 collective-permute-done.31.refs_5_.refs_3_
  129.5 1.3 collective-permute-start.32
  132.2 3.3 %collective-permute-done.32.refs_1_.refs_4_ = bf16[2,96,768]{2,1,0:T(8,128)(2,1)S(1)} collective-permute-done((bf16[2,96,768]{2,1,0:T(8,128)(2,1)S(1)}, bf16[2,96,768]{2,1,0:T(8,128)(2,1)S(1)}, u32[]{:S(2)}, u32[]{:S(2)}) %collective-permute-start.32) | collective-permute-done | bytes 294944 | tf_op jit(solution)/shard_map/ppermute | solution.py:56
  136.5 2.3 %collective-permute-start.38 = (bf16[96,768]{1,0:T(8,128)(2,1)S(1)}, bf16[96,768]{1,0:T(8,128)(2,1)S(1)}, u32[]{:S(2)}, u32[]{:S(2)}) collective-permute-start(bf16[96,768]{1,0:T(8,128)(2,1)S(1)} %far_back.1.refs_4_), channel_id=1, source_target_pairs={{0,2},{1,3},{2,0},{3,1},{4,6},{5,7},{6,4},{7,5},{8,10},{9,11},{10,... | collective-permute-start | bytes 442376 | tf_op jit(solution)/shard_map/ppermute | solution.py:56
  139.2 3.2 %collective-permute-done.37.refs_5_ = bf16[2,96,768]{2,1,0:T(8,128)(2,1)S(1)} collective-permute-done((bf16[2,96,768]{2,1,0:T(8,128)(2,1)S(1)}, bf16[2,96,768]{2,1,0:T(8,128)(2,1)S(1)}, u32[]{:S(2)}, u32[]{:S(2)}) %collective-permute-start.37) | collective-permute-done | bytes 294944 | tf_op jit(solution)/shard_map/ppermute | solution.py:56
  143.9 1.6 collective-permute-done.35.refs_5_
  145.7 2.2 collective-permute-start.39
  148.1 16.6 %collective-permute-done.40.refs_1_ = bf16[2,96,768]{2,1,0:T(8,128)(2,1)S(1)} collective-permute-done((bf16[2,96,768]{2,1,0:T(8,128)(2,1)S(1)}, bf16[2,96,768]{2,1,0:T(8,128)(2,1)S(1)}, u32[]{:S(2)}, u32[]{:S(2)}) %collective-permute-start.40) | collective-permute-done | bytes 294944 | tf_op jit(solution)/shard_map/ppermute | solution.py:56
  166.7 2.6 %collective-permute-start.47 = (bf16[96,768]{1,0:T(8,128)(2,1)S(1)}, bf16[96,768]{1,0:T(8,128)(2,1)S(1)}, u32[]{:S(2)}, u32[]{:S(2)}) collective-permute-start(bf16[96,768]{1,0:T(8,128)(2,1)S(1)} %far_in.1.refs_2_), channel_id=1, source_target_pairs={{0,2},{1,3},{2,0},{3,1},{4,6},{5,7},{6,4},{7,5},{8,10},{9,11},{10,... | collective-permute-start | bytes 442376 | tf_op jit(solution)/shard_map/ppermute | solution.py:56
  169.3 2.2 collective-permute-done.44.refs_1_.refs_3_
  171.5 2.4 %collective-permute-done.42.refs_2_.refs_1_ = bf16[208,768]{1,0:T(8,128)(2,1)S(1)} collective-permute-done((bf16[208,768]{1,0:T(8,128)(2,1)S(1)}, bf16[208,768]{1,0:T(8,128)(2,1)S(1)}, u32[]{:S(2)}, u32[]{:S(2)}) %collective-permute-start.42) | collective-permute-done | bytes 319520 | tf_op jit(solution)/shard_map/ppermute | solution.py:56
  174.0 1.6 collective-permute-start.45
  175.7 1.5 collective-permute-start.49
  177.4 9.6 %collective-permute-start.52 = (bf16[256,768]{1,0:T(8,128)(2,1)S(1)}, bf16[256,768]{1,0:T(8,128)(2,1)S(1)}, u32[]{:S(2)}, u32[]{:S(2)}) collective-permute-start(bf16[256,768]{1,0:T(8,128)(2,1)S(1)} %get-tuple-element.181), channel_id=1, source_target_pairs={{0,0},{1,1},{2,4},{3,5},{4,2},{5,3},{6,6},{7,7},{8,8},{9,9},{10,12... | collective-permute-start | bytes 1179656 | tf_op jit(solution)/shard_map/ppermute | solution.py:67
  187.0 10.5 %collective-permute-start.53 = (bf16[256,768]{1,0:T(8,128)(2,1)S(1)}, bf16[256,768]{1,0:T(8,128)(2,1)S(1)}, u32[]{:S(2)}, u32[]{:S(2)}) collective-permute-start(bf16[256,768]{1,0:T(8,128)(2,1)S(1)} %get-tuple-element.182), channel_id=1, source_target_pairs={{0,0},{1,1},{2,4},{3,5},{4,2},{5,3},{6,6},{7,7},{8,8},{9,9},{10,12... | collective-permute-start | bytes 1179656 | tf_op jit(solution)/shard_map/ppermute | solution.py:67
  199.2 7.5 %collective-permute-done.53.refs_12_.low_out = bf16[256,768]{1,0:T(8,128)(2,1)S(1)} collective-permute-done((bf16[256,768]{1,0:T(8,128)(2,1)S(1)}, bf16[256,768]{1,0:T(8,128)(2,1)S(1)}, u32[]{:S(2)}, u32[]{:S(2)}) %collective-permute-start.53) | collective-permute-done | bytes 393248 | tf_op jit(solution)/shard_map/ppermute | solution.py:67
  207.1 3.6 %first_half.1 = (f32[768,2304]{1,0:T(8,128)}, f32[768,768]{1,0:T(8,128)}, f32[768,768]{1,0:T(8,128)}, bf16[256,768]{1,0:T(8,128)(2,1)}, bf16[256,768]{1,0:T(8,128)(2,1)}) custom-call(s32[5]{0:T(128)S(1)} %stack.27.refs_0_.info, bf16[2320,768]{1,0:T(8,128)(2,1)S(1)} %plane.1, bf16[256,768]{1,0:T(8,128)(2,1)S(1)} %collective-permute-done.52.refs_11_.low_tokens, ...), custom_call_target="tpu_custom_call" | custom-call | flops 1 | bytes 1 | tf_op jit(solution)/shard_map/first_half/pallas_call | solution.py:1068
  210.7 2.6 %collective-permute-done.54.other = bf16[2320,768]{1,0:T(8,128)(2,1)S(1)} collective-permute-done((bf16[2320,768]{1,0:T(8,128)(2,1)S(1)}, bf16[2320,768]{1,0:T(8,128)(2,1)S(1)}, u32[]{:S(2)}, u32[]{:S(2)}) %collective-permute-start.54) | collective-permute-done | bytes 3563552 | tf_op jit(solution)/shard_map/ppermute | solution.py:56
  213.3 4.9 %second_half.1 = (f32[768,2304]{1,0:T(8,128)}, f32[768,768]{1,0:T(8,128)}, f32[768,768]{1,0:T(8,128)}, f32[768,768]{1,0:T(8,128)}, f32[768]{0:T(1024)}, /*index=...) custom-call(s32[5]{0:T(128)S(1)} %stack.27.refs_0_.info, ...), custom_call_target="tpu_custom_call", output_to_operand_aliasing={{0}: (3, {}), {1}: (4, {}), {2}: (5, {})} | custom-call | flops 1 | bytes 1 | tf_op jit(solution)/shard_map/second_half/pallas_call | solution.py:1078
  (141 shorter events, 28.1 us)
Async XLA Ops:
  0.7 26.7 %collective-permute-start = (bf16[256,768]{1,0:T(8,128)(2,1)}, bf16[256,768]{1,0:T(8,128)(2,1)S(1)}, u32[]{:S(2)}, u32[]{:S(2)}) collective-permute-start(bf16[256,768]{1,0:T(8,128)(2,1)} %bitcast.11), channel_id=1, source_target_pairs={{0,0},{1,1},{2,4},{3,5},{4,2},{5,3},{6,6},{7,7},{8,8},{9,9},{10,12... | collective-permute-start | bytes 1179656 | tf_op jit(solution)/shard_map/ppermute | solution.py:67
  10.9 16.5 %collective-permute-start.6 = (bf16[208,768]{1,0:T(8,128)(2,1)S(1)}, bf16[208,768]{1,0:T(8,128)(2,1)S(1)}, u32[]{:S(2)}, u32[]{:S(2)}) collective-permute-start(bf16[208,768]{1,0:T(8,128)(2,1)S(1)} %piece.1), channel_id=1, source_target_pairs={{0,2},{1,3},{2,0},{3,1},{4,6},{5,7},{6,4},{7,5},{8,10},{9,11},{10,... | collective-permute-start | bytes 958472 | tf_op jit(solution)/shard_map/ppermute | solution.py:56
  11.0 16.4 %collective-permute-start.5 = (bf16[208,768]{1,0:T(8,128)(2,1)S(1)}, bf16[208,768]{1,0:T(8,128)(2,1)S(1)}, u32[]{:S(2)}, u32[]{:S(2)}) collective-permute-start(bf16[208,768]{1,0:T(8,128)(2,1)S(1)} %piece.1), channel_id=1, source_target_pairs={{0,1},{1,0},{2,3},{3,2},{4,5},{5,4},{6,7},{7,6},{8,9},{9,8},{10,11... | collective-permute-start | bytes 958472 | tf_op jit(solution)/shard_map/ppermute | solution.py:56
  27.4 20.2 %collective-permute-start.8 = (bf16[416,768]{1,0:T(8,128)(2,1)S(1)}, bf16[416,768]{1,0:T(8,128)(2,1)S(1)}, u32[]{:S(2)}, u32[]{:S(2)}) collective-permute-start(bf16[416,768]{1,0:T(8,128)(2,1)S(1)} %pair.1.refs_0_), channel_id=1, source_target_pairs={{0,16},{1,17},{2,18},{3,19},{4,20},{5,21},{6,22},{7,23},{8,24},{9,... | collective-permute-start | bytes 1916936 | tf_op jit(solution)/shard_map/ppermute | solution.py:56
  28.7 18.9 %collective-permute-start.7 = (bf16[416,768]{1,0:T(8,128)(2,1)S(1)}, bf16[416,768]{1,0:T(8,128)(2,1)S(1)}, u32[]{:S(2)}, u32[]{:S(2)}) collective-permute-start(bf16[416,768]{1,0:T(8,128)(2,1)S(1)} %pair.1.refs_0_), channel_id=1, source_target_pairs={{0,8},{1,9},{2,10},{3,11},{4,12},{5,13},{6,14},{7,15},{8,0},{9,1},... | collective-permute-start | bytes 1916936 | tf_op jit(solution)/shard_map/ppermute | solution.py:56
  29.9 17.7 %collective-permute-start.1 = (bf16[256,768]{1,0:T(8,128)(2,1)S(1)}, bf16[256,768]{1,0:T(8,128)(2,1)S(1)}, u32[]{:S(2)}, u32[]{:S(2)}) collective-permute-start(bf16[256,768]{1,0:T(8,128)(2,1)S(1)} %collective-permute-done.refs_2_.refs_3_.refs_0_.refs_1_), channel_id=1, source_target_pairs={{0,1},{1,0},{2,3},{3,2},{4,5},{5,4},{6,7},{7,6},{8,9},{9,8},{10,11... | collective-permute-start | bytes 1179656 | tf_op jit(solution)/shard_map/ppermute | solution.py:56
  33.0 14.6 %collective-permute-start.9 = (bf16[208,768]{1,0:T(8,128)(2,1)S(1)}, bf16[208,768]{1,0:T(8,128)(2,1)S(1)}, u32[]{:S(2)}, u32[]{:S(2)}) collective-permute-start(bf16[208,768]{1,0:T(8,128)(2,1)S(1)} %collective-permute-done.6.refs_1_), channel_id=1, source_target_pairs={{0,1},{1,0},{2,3},{3,2},{4,5},{5,4},{6,7},{7,6},{8,9},{9,8},{10,11... | collective-permute-start | bytes 958472 | tf_op jit(solution)/shard_map/ppermute | solution.py:56
  47.7 18.6 %collective-permute-start.11 = (bf16[432,768]{1,0:T(8,128)(2,1)S(1)}, bf16[432,768]{1,0:T(8,128)(2,1)S(1)}, u32[]{:S(2)}, u32[]{:S(2)}) collective-permute-start(bf16[432,768]{1,0:T(8,128)(2,1)S(1)} %get-tuple-element.110.refs_9_), channel_id=1, source_target_pairs={{0,8},{1,9},{2,10},{3,11},{4,12},{5,13},{6,14},{7,15},{8,0},{9,1},... | collective-permute-start | bytes 1990664 | tf_op jit(solution)/shard_map/ppermute | solution.py:56
  48.0 18.2 %collective-permute-start.12 = (bf16[400,768]{1,0:T(8,128)(2,1)S(1)}, bf16[400,768]{1,0:T(8,128)(2,1)S(1)}, u32[]{:S(2)}, u32[]{:S(2)}) collective-permute-start(bf16[400,768]{1,0:T(8,128)(2,1)S(1)} %get-tuple-element.112), channel_id=1, source_target_pairs={{0,16},{1,17},{2,18},{3,19},{4,20},{5,21},{6,22},{7,23},{8,24},{9,... | collective-permute-start | bytes 1843208 | tf_op jit(solution)/shard_map/ppermute | solution.py:56
  48.2 6.7 %collective-permute-start.2 = (bf16[256,768]{1,0:T(8,128)(2,1)S(1)}, bf16[256,768]{1,0:T(8,128)(2,1)S(1)}, u32[]{:S(2)}, u32[]{:S(2)}) collective-permute-start(bf16[256,768]{1,0:T(8,128)(2,1)S(1)} %collective-permute-done.refs_2_.refs_3_.refs_0_.refs_1_), channel_id=1, source_target_pairs={{0,4},{1,5},{2,6},{3,7},{4,0},{5,1},{6,2},{7,3},{8,12},{9,13},{10,... | collective-permute-start | bytes 1179656 | tf_op jit(solution)/shard_map/ppermute | solution.py:56
  51.1 14.2 %collective-permute-start.14 = (bf16[256,768]{1,0:T(8,128)(2,1)S(1)}, bf16[256,768]{1,0:T(8,128)(2,1)S(1)}, u32[]{:S(2)}, u32[]{:S(2)}) collective-permute-start(bf16[256,768]{1,0:T(8,128)(2,1)S(1)} %bitcast.12), channel_id=1, source_target_pairs={{0,0},{1,1},{2,4},{3,5},{4,2},{5,3},{6,6},{7,7},{8,8},{9,9},{10,12... | collective-permute-start | bytes 1179656 | tf_op jit(solution)/shard_map/ppermute | solution.py:67
  66.5 9.4 %collective-permute-start.16 = (bf16[2288,768]{1,0:T(8,128)(2,1)S(1)}, bf16[2288,768]{1,0:T(8,128)(2,1)S(1)}, u32[]{:S(2)}, u32[]{:S(2)}) collective-permute-start(bf16[2288,768]{1,0:T(8,128)(2,1)S(1)} %held.1.refs_5_.refs_1_), channel_id=1, source_target_pairs={{0,4},{1,5},{2,6},{3,7},{4,0},{5,1},{6,2},{7,3},{8,12},{9,13},{10,... | collective-permute-start | bytes 10543112 | tf_op jit(solution)/shard_map/ppermute | solution.py:56
  66.7 6.1 %collective-permute-start.10 = (bf16[768,128]{1,0:T(8,128)(2,1)S(1)}, bf16[768,128]{1,0:T(8,128)(2,1)S(1)}, u32[]{:S(2)}, u32[]{:S(2)}) collective-permute-start(bf16[768,128]{1,0:T(8,128)(2,1)S(1)} %get-tuple-element.111), channel_id=1, source_target_pairs={{0,1},{1,0},{2,3},{3,2},{4,5},{5,4},{6,7},{7,6},{8,9},{9,8},{10,11... | collective-permute-start | bytes 589832 | tf_op jit(solution)/shard_map/ppermute | solution.py:56
  67.6 5.8 %collective-permute-start.18 = (bf16[112,768]{1,0:T(8,128)(2,1)S(1)}, bf16[112,768]{1,0:T(8,128)(2,1)S(1)}, u32[]{:S(2)}, u32[]{:S(2)}) collective-permute-start(bf16[112,768]{1,0:T(8,128)(2,1)S(1)} %get-tuple-element.120), channel_id=1, source_target_pairs={{0,8},{1,9},{2,10},{3,11},{4,12},{5,13},{6,14},{7,15},{8,0},{9,1},... | collective-permute-start | bytes 516104 | tf_op jit(solution)/shard_map/ppermute | solution.py:56
  85.0 6.6 %collective-permute-start.23 = (bf16[2,4,2,96,768]{4,3,2,1,0:T(8,128)(2,1)S(1)}, bf16[2,4,2,96,768]{4,3,2,1,0:T(8,128)(2,1)S(1)}, u32[]{:S(2)}, u32[]{:S(2)}) collective-permute-start(bf16[2,4,2,96,768]{4,3,2,1,0:T(8,128)(2,1)S(1)} %get-tuple-element.140), channel_id=1, source_target_pairs={{0,4},{1,5},{2,6},{3,7},{4,0},{5,1},{6,2},{7,3},{8,12},{9,13},{10,... | collective-permute-start | bytes 7077896 | tf_op jit(solution)/shard_map/ppermute | solution.py:56
  91.0 17.0 %collective-permute-start.24 = (bf16[2,4,2,96,768]{4,3,2,1,0:T(8,128)(2,1)S(1)}, bf16[2,4,2,96,768]{4,3,2,1,0:T(8,128)(2,1)S(1)}, u32[]{:S(2)}, u32[]{:S(2)}) collective-permute-start(bf16[2,4,2,96,768]{4,3,2,1,0:T(8,128)(2,1)S(1)} %get-tuple-element.147), channel_id=1, source_target_pairs={{0,4},{1,5},{2,6},{3,7},{4,0},{5,1},{6,2},{7,3},{8,12},{9,13},{10,... | collective-permute-start | bytes 7077896 | tf_op jit(solution)/shard_map/ppermute | solution.py:56
  91.2 6.8 %collective-permute-start.22 = (bf16[768,384]{1,0:T(8,128)(2,1)S(1)}, bf16[768,384]{1,0:T(8,128)(2,1)S(1)}, u32[]{:S(2)}, u32[]{:S(2)}) collective-permute-start(bf16[768,384]{1,0:T(8,128)(2,1)S(1)} %get-tuple-element.138), channel_id=1, source_target_pairs={{0,4},{1,5},{2,6},{3,7},{4,0},{5,1},{6,2},{7,3},{8,12},{9,13},{10,... | collective-permute-start | bytes 1769480 | tf_op jit(solution)/shard_map/ppermute | solution.py:56
  91.9 16.2 %collective-permute-start.26 = (bf16[2,2,96,768]{3,2,1,0:T(8,128)(2,1)S(1)}, bf16[2,2,96,768]{3,2,1,0:T(8,128)(2,1)S(1)}, u32[]{:S(2)}, u32[]{:S(2)}) collective-permute-start(bf16[2,2,96,768]{3,2,1,0:T(8,128)(2,1)S(1)} %get-tuple-element.148), channel_id=1, source_target_pairs={{0,16},{1,17},{2,18},{3,19},{4,20},{5,21},{6,22},{7,23},{8,24},{9,... | collective-permute-start | bytes 1769480 | tf_op jit(solution)/shard_map/ppermute | solution.py:56
  93.2 14.9 %collective-permute-start.25 = (bf16[2,2,96,768]{3,2,1,0:T(8,128)(2,1)S(1)}, bf16[2,2,96,768]{3,2,1,0:T(8,128)(2,1)S(1)}, u32[]{:S(2)}, u32[]{:S(2)}) collective-permute-start(bf16[2,2,96,768]{3,2,1,0:T(8,128)(2,1)S(1)} %get-tuple-element.141.refs_11_), channel_id=1, source_target_pairs={{0,8},{1,9},{2,10},{3,11},{4,12},{5,13},{6,14},{7,15},{8,0},{9,1},... | collective-permute-start | bytes 1769480 | tf_op jit(solution)/shard_map/ppermute | solution.py:56
  96.8 6.4 %collective-permute-start.21 = (bf16[768,128]{1,0:T(8,128)(2,1)S(1)}, bf16[768,128]{1,0:T(8,128)(2,1)S(1)}, u32[]{:S(2)}, u32[]{:S(2)}) collective-permute-start(bf16[768,128]{1,0:T(8,128)(2,1)S(1)} %to_z.1), channel_id=1, source_target_pairs={{0,1},{1,0},{2,3},{3,2},{4,5},{5,4},{6,7},{7,6},{8,9},{9,8},{10,11... | collective-permute-start | bytes 589832 | tf_op jit(solution)/shard_map/ppermute | solution.py:56
  98.4 21.8 %collective-permute-start.27 = (bf16[768,192]{1,0:T(8,128)(2,1)S(1)}, bf16[768,192]{1,0:T(8,128)(2,1)S(1)}, u32[]{:S(2)}, u32[]{:S(2)}) collective-permute-start(bf16[768,192]{1,0:T(8,128)(2,1)S(1)} %get-tuple-element.155), channel_id=1, source_target_pairs={{0,1},{1,0},{2,3},{3,2},{4,5},{5,4},{6,7},{7,6},{8,9},{9,8},{10,11... | collective-permute-start | bytes 884744 | tf_op jit(solution)/shard_map/ppermute | solution.py:56
  108.6 19.7 %collective-permute-start.31 = (bf16[6,96,768]{2,1,0:T(8,128)(2,1)S(1)}, bf16[6,96,768]{2,1,0:T(8,128)(2,1)S(1)}, u32[]{:S(2)}, u32[]{:S(2)}) collective-permute-start(bf16[6,96,768]{2,1,0:T(8,128)(2,1)S(1)} %get-tuple-element.164), channel_id=1, source_target_pairs={{0,16},{1,17},{2,18},{3,19},{4,20},{5,21},{6,22},{7,23},{8,24},{9,... | collective-permute-start | bytes 2654216 | tf_op jit(solution)/shard_map/ppermute | solution.py:56
  109.9 19.3 %collective-permute-start.30 = (bf16[6,96,768]{2,1,0:T(8,128)(2,1)S(1)}, bf16[6,96,768]{2,1,0:T(8,128)(2,1)S(1)}, u32[]{:S(2)}, u32[]{:S(2)}) collective-permute-start(bf16[6,96,768]{2,1,0:T(8,128)(2,1)S(1)} %get-tuple-element.149.refs_10_), channel_id=1, source_target_pairs={{0,8},{1,9},{2,10},{3,11},{4,12},{5,13},{6,14},{7,15},{8,0},{9,1},... | collective-permute-start | bytes 2654216 | tf_op jit(solution)/shard_map/ppermute | solution.py:56
  123.8 7.9 %collective-permute-start.33 = (bf16[512,768]{1,0:T(8,128)(2,1)S(1)}, bf16[512,768]{1,0:T(8,128)(2,1)S(1)}, u32[]{:S(2)}, u32[]{:S(2)}) collective-permute-start(bf16[512,768]{1,0:T(8,128)(2,1)S(1)} %get-tuple-element.168), channel_id=1, source_target_pairs={{0,4},{1,5},{2,6},{3,7},{4,0},{5,1},{6,2},{7,3},{8,12},{9,13},{10,... | collective-permute-start | bytes 2359304 | tf_op jit(solution)/shard_map/ppermute | solution.py:56
  126.0 10.1 %collective-permute-start.28 = (bf16[416,384]{1,0:T(8,128)(2,1)S(1)}, bf16[416,384]{1,0:T(8,128)(2,1)S(1)}, u32[]{:S(2)}, u32[]{:S(2)}) collective-permute-start(bf16[416,384]{1,0:T(8,128)(2,1)S(1)} %get-tuple-element.161), channel_id=1, source_target_pairs={{0,8},{1,9},{2,10},{3,11},{4,12},{5,13},{6,14},{7,15},{8,0},{9,1},... | collective-permute-start | bytes 958472 | tf_op jit(solution)/shard_map/ppermute | solution.py:56
  126.3 9.8 %collective-permute-start.29 = (bf16[416,384]{1,0:T(8,128)(2,1)S(1)}, bf16[416,384]{1,0:T(8,128)(2,1)S(1)}, u32[]{:S(2)}, u32[]{:S(2)}) collective-permute-start(bf16[416,384]{1,0:T(8,128)(2,1)S(1)} %get-tuple-element.163), channel_id=1, source_target_pairs={{0,16},{1,17},{2,18},{3,19},{4,20},{5,21},{6,22},{7,23},{8,24},{9,... | collective-permute-start | bytes 958472 | tf_op jit(solution)/shard_map/ppermute | solution.py:56
  129.5 5.9 %collective-permute-start.32 = (bf16[2,96,768]{2,1,0:T(8,128)(2,1)S(1)}, bf16[2,96,768]{2,1,0:T(8,128)(2,1)S(1)}, u32[]{:S(2)}, u32[]{:S(2)}) collective-permute-start(bf16[2,96,768]{2,1,0:T(8,128)(2,1)S(1)} %get-tuple-element.167), channel_id=1, source_target_pairs={{0,1},{1,0},{2,3},{3,2},{4,5},{5,4},{6,7},{7,6},{8,9},{9,8},{10,11... | collective-permute-start | bytes 884744 | tf_op jit(solution)/shard_map/ppermute | solution.py:56
  131.0 11.4 %collective-permute-start.37 = (bf16[2,96,768]{2,1,0:T(8,128)(2,1)S(1)}, bf16[2,96,768]{2,1,0:T(8,128)(2,1)S(1)}, u32[]{:S(2)}, u32[]{:S(2)}) collective-permute-start(bf16[2,96,768]{2,1,0:T(8,128)(2,1)S(1)} %get-tuple-element.172), channel_id=1, source_target_pairs={{0,8},{1,9},{2,10},{3,11},{4,12},{5,13},{6,14},{7,15},{8,0},{9,1},... | collective-permute-start | bytes 884744 | tf_op jit(solution)/shard_map/ppermute | solution.py:56
  131.8 11.8 %collective-permute-start.36 = (bf16[2,96,768]{2,1,0:T(8,128)(2,1)S(1)}, bf16[2,96,768]{2,1,0:T(8,128)(2,1)S(1)}, u32[]{:S(2)}, u32[]{:S(2)}) collective-permute-start(bf16[2,96,768]{2,1,0:T(8,128)(2,1)S(1)} %get-tuple-element.169.refs_2_), channel_id=1, source_target_pairs={{0,16},{1,17},{2,18},{3,19},{4,20},{5,21},{6,22},{7,23},{8,24},{9,... | collective-permute-start | bytes 884744 | tf_op jit(solution)/shard_map/ppermute | solution.py:56
  136.2 9.4 %collective-permute-start.34 = (bf16[224,384]{1,0:T(8,128)(2,1)S(1)}, bf16[224,384]{1,0:T(8,128)(2,1)S(1)}, u32[]{:S(2)}, u32[]{:S(2)}) collective-permute-start(bf16[224,384]{1,0:T(8,128)(2,1)S(1)} %get-tuple-element.170.refs_6_), channel_id=1, source_target_pairs={{0,16},{1,17},{2,18},{3,19},{4,20},{5,21},{6,22},{7,23},{8,24},{9,... | collective-permute-start | bytes 516104 | tf_op jit(solution)/shard_map/ppermute | solution.py:56
  136.5 7.4 %collective-permute-start.38 = (bf16[96,768]{1,0:T(8,128)(2,1)S(1)}, bf16[96,768]{1,0:T(8,128)(2,1)S(1)}, u32[]{:S(2)}, u32[]{:S(2)}) collective-permute-start(bf16[96,768]{1,0:T(8,128)(2,1)S(1)} %far_back.1.refs_4_), channel_id=1, source_target_pairs={{0,2},{1,3},{2,0},{3,1},{4,6},{5,7},{6,4},{7,5},{8,10},{9,11},{10,... | collective-permute-start | bytes 442376 | tf_op jit(solution)/shard_map/ppermute | solution.py:56
  138.8 6.7 %collective-permute-start.35 = (bf16[192,384]{1,0:T(8,128)(2,1)S(1)}, bf16[192,384]{1,0:T(8,128)(2,1)S(1)}, u32[]{:S(2)}, u32[]{:S(2)}) collective-permute-start(bf16[192,384]{1,0:T(8,128)(2,1)S(1)} %get-tuple-element.171), channel_id=1, source_target_pairs={{0,8},{1,9},{2,10},{3,11},{4,12},{5,13},{6,14},{7,15},{8,0},{9,1},... | collective-permute-start | bytes 442376 | tf_op jit(solution)/shard_map/ppermute | solution.py:56
  142.4 22.4 %collective-permute-start.41 = (bf16[256,768]{1,0:T(8,128)(2,1)S(1)}, bf16[256,768]{1,0:T(8,128)(2,1)S(1)}, u32[]{:S(2)}, u32[]{:S(2)}) collective-permute-start(bf16[256,768]{1,0:T(8,128)(2,1)S(1)} %near.1.refs_2_), channel_id=1, source_target_pairs={{0,1},{1,0},{2,3},{3,2},{4,5},{5,4},{6,7},{7,6},{8,9},{9,8},{10,11... | collective-permute-start | bytes 1179656 | tf_op jit(solution)/shard_map/ppermute | solution.py:56
  145.7 19.1 %collective-permute-start.39 = (bf16[208,768]{1,0:T(8,128)(2,1)S(1)}, bf16[208,768]{1,0:T(8,128)(2,1)S(1)}, u32[]{:S(2)}, u32[]{:S(2)}) collective-permute-start(bf16[208,768]{1,0:T(8,128)(2,1)S(1)} %qkv_three.1.refs_2_.refs_0_), channel_id=1, source_target_pairs={{0,2},{1,3},{2,0},{3,1},{4,6},{5,7},{6,4},{7,5},{8,10},{9,11},{10,... | collective-permute-start | bytes 958472 | tf_op jit(solution)/shard_map/ppermute | solution.py:56
  147.9 16.9 %collective-permute-start.40 = (bf16[2,96,768]{2,1,0:T(8,128)(2,1)S(1)}, bf16[2,96,768]{2,1,0:T(8,128)(2,1)S(1)}, u32[]{:S(2)}, u32[]{:S(2)}) collective-permute-start(bf16[2,96,768]{2,1,0:T(8,128)(2,1)S(1)} %get-tuple-element.174), channel_id=1, source_target_pairs={{0,1},{1,0},{2,3},{3,2},{4,5},{5,4},{6,7},{7,6},{8,9},{9,8},{10,11... | collective-permute-start | bytes 884744 | tf_op jit(solution)/shard_map/ppermute | solution.py:56
  164.9 9.0 %collective-permute-start.42 = (bf16[208,768]{1,0:T(8,128)(2,1)S(1)}, bf16[208,768]{1,0:T(8,128)(2,1)S(1)}, u32[]{:S(2)}, u32[]{:S(2)}) collective-permute-start(bf16[208,768]{1,0:T(8,128)(2,1)S(1)} %qkv_four.1.refs_0_), channel_id=1, source_target_pairs={{0,1},{1,0},{2,3},{3,2},{4,5},{5,4},{6,7},{7,6},{8,9},{9,8},{10,11... | collective-permute-start | bytes 958472 | tf_op jit(solution)/shard_map/ppermute | solution.py:56
  165.8 5.6 %collective-permute-start.44 = (bf16[192,768]{1,0:T(8,128)(2,1)S(1)}, bf16[192,768]{1,0:T(8,128)(2,1)S(1)}, u32[]{:S(2)}, u32[]{:S(2)}) collective-permute-start(bf16[192,768]{1,0:T(8,128)(2,1)S(1)} %slice.9), channel_id=1, source_target_pairs={{0,16},{1,17},{2,18},{3,19},{4,20},{5,21},{6,22},{7,23},{8,24},{9,... | collective-permute-start | bytes 884744 | tf_op jit(solution)/shard_map/ppermute | solution.py:56
  165.9 5.6 %collective-permute-start.43 = (bf16[192,768]{1,0:T(8,128)(2,1)S(1)}, bf16[192,768]{1,0:T(8,128)(2,1)S(1)}, u32[]{:S(2)}, u32[]{:S(2)}) collective-permute-start(bf16[192,768]{1,0:T(8,128)(2,1)S(1)} %slice.9), channel_id=1, source_target_pairs={{0,8},{1,9},{2,10},{3,11},{4,12},{5,13},{6,14},{7,15},{8,0},{9,1},... | collective-permute-start | bytes 884744 | tf_op jit(solution)/shard_map/ppermute | solution.py:56
  166.7 9.0 %collective-permute-start.47 = (bf16[96,768]{1,0:T(8,128)(2,1)S(1)}, bf16[96,768]{1,0:T(8,128)(2,1)S(1)}, u32[]{:S(2)}, u32[]{:S(2)}) collective-permute-start(bf16[96,768]{1,0:T(8,128)(2,1)S(1)} %far_in.1.refs_2_), channel_id=1, source_target_pairs={{0,2},{1,3},{2,0},{3,1},{4,6},{5,7},{6,4},{7,5},{8,10},{9,11},{10,... | collective-permute-start | bytes 442376 | tf_op jit(solution)/shard_map/ppermute | solution.py:56
  173.9 23.6 %collective-permute-start.46 = (bf16[288,768]{1,0:T(8,128)(2,1)S(1)}, bf16[288,768]{1,0:T(8,128)(2,1)S(1)}, u32[]{:S(2)}, u32[]{:S(2)}) collective-permute-start(bf16[288,768]{1,0:T(8,128)(2,1)S(1)} %get-tuple-element.176), channel_id=1, source_target_pairs={{0,16},{1,17},{2,18},{3,19},{4,20},{5,21},{6,22},{7,23},{8,24},{9,... | collective-permute-start | bytes 1327112 | tf_op jit(solution)/shard_map/ppermute | solution.py:56
  174.0 23.5 %collective-permute-start.45 = (bf16[288,768]{1,0:T(8,128)(2,1)S(1)}, bf16[288,768]{1,0:T(8,128)(2,1)S(1)}, u32[]{:S(2)}, u32[]{:S(2)}) collective-permute-start(bf16[288,768]{1,0:T(8,128)(2,1)S(1)} %get-tuple-element.175.refs_6_), channel_id=1, source_target_pairs={{0,8},{1,9},{2,10},{3,11},{4,12},{5,13},{6,14},{7,15},{8,0},{9,1},... | collective-permute-start | bytes 1327112 | tf_op jit(solution)/shard_map/ppermute | solution.py:56
  175.7 11.2 %collective-permute-start.49 = (bf16[2,96,768]{2,1,0:T(8,128)(2,1)S(1)}, bf16[2,96,768]{2,1,0:T(8,128)(2,1)S(1)}, u32[]{:S(2)}, u32[]{:S(2)}) collective-permute-start(bf16[2,96,768]{2,1,0:T(8,128)(2,1)S(1)} %last.1.refs_5_.refs_6_), channel_id=1, source_target_pairs={{0,16},{1,17},{2,18},{3,19},{4,20},{5,21},{6,22},{7,23},{8,24},{9,... | collective-permute-start | bytes 884744 | tf_op jit(solution)/shard_map/ppermute | solution.py:56
  177.2 20.3 %collective-permute-start.48 = (bf16[2,96,768]{2,1,0:T(8,128)(2,1)S(1)}, bf16[2,96,768]{2,1,0:T(8,128)(2,1)S(1)}, u32[]{:S(2)}, u32[]{:S(2)}) collective-permute-start(bf16[2,96,768]{2,1,0:T(8,128)(2,1)S(1)} %last.1.refs_5_.refs_6_), channel_id=1, source_target_pairs={{0,8},{1,9},{2,10},{3,11},{4,12},{5,13},{6,14},{7,15},{8,0},{9,1},... | collective-permute-start | bytes 884744 | tf_op jit(solution)/shard_map/ppermute | solution.py:56
  177.4 21.8 %collective-permute-start.52 = (bf16[256,768]{1,0:T(8,128)(2,1)S(1)}, bf16[256,768]{1,0:T(8,128)(2,1)S(1)}, u32[]{:S(2)}, u32[]{:S(2)}) collective-permute-start(bf16[256,768]{1,0:T(8,128)(2,1)S(1)} %get-tuple-element.181), channel_id=1, source_target_pairs={{0,0},{1,1},{2,4},{3,5},{4,2},{5,3},{6,6},{7,7},{8,8},{9,9},{10,12... | collective-permute-start | bytes 1179656 | tf_op jit(solution)/shard_map/ppermute | solution.py:67
  187.0 19.8 %collective-permute-start.53 = (bf16[256,768]{1,0:T(8,128)(2,1)S(1)}, bf16[256,768]{1,0:T(8,128)(2,1)S(1)}, u32[]{:S(2)}, u32[]{:S(2)}) collective-permute-start(bf16[256,768]{1,0:T(8,128)(2,1)S(1)} %get-tuple-element.182), channel_id=1, source_target_pairs={{0,0},{1,1},{2,4},{3,5},{4,2},{5,3},{6,6},{7,7},{8,8},{9,9},{10,12... | collective-permute-start | bytes 1179656 | tf_op jit(solution)/shard_map/ppermute | solution.py:67
  197.6 9.2 %collective-permute-start.50 = (bf16[192,768]{1,0:T(8,128)(2,1)S(1)}, bf16[192,768]{1,0:T(8,128)(2,1)S(1)}, u32[]{:S(2)}, u32[]{:S(2)}) collective-permute-start(bf16[192,768]{1,0:T(8,128)(2,1)S(1)} %get-tuple-element.177), channel_id=1, source_target_pairs={{0,8},{1,9},{2,10},{3,11},{4,12},{5,13},{6,14},{7,15},{8,0},{9,1},... | collective-permute-start | bytes 884744 | tf_op jit(solution)/shard_map/ppermute | solution.py:56
  198.7 8.1 %collective-permute-start.51 = (bf16[192,768]{1,0:T(8,128)(2,1)S(1)}, bf16[192,768]{1,0:T(8,128)(2,1)S(1)}, u32[]{:S(2)}, u32[]{:S(2)}) collective-permute-start(bf16[192,768]{1,0:T(8,128)(2,1)S(1)} %get-tuple-element.178), channel_id=1, source_target_pairs={{0,16},{1,17},{2,18},{3,19},{4,20},{5,21},{6,22},{7,23},{8,24},{9,... | collective-permute-start | bytes 884744 | tf_op jit(solution)/shard_map/ppermute | solution.py:56
  207.0 6.3 %collective-permute-start.54 = (bf16[2320,768]{1,0:T(8,128)(2,1)S(1)}, bf16[2320,768]{1,0:T(8,128)(2,1)S(1)}, u32[]{:S(2)}, u32[]{:S(2)}) collective-permute-start(bf16[2320,768]{1,0:T(8,128)(2,1)S(1)} %plane.1), channel_id=1, source_target_pairs={{0,4},{1,5},{2,6},{3,7},{4,0},{5,1},{6,2},{7,3},{8,12},{9,13},{10,... | collective-permute-start | bytes 10690568 | tf_op jit(solution)/shard_map/ppermute | solution.py:56
  (25 other events, 121.9 us)
